TPU v7x, 128 devices: a whole 4x4x4 slice. The times are simulated.
128 devices in a mesh: seq: 32 (over x, z, core), wt: 4 (over y).
Axes of the slice: x: 4, y: 4, z: 4, core: 2. Of those that a mesh axis runs over, the one named last changes fastest.
Arguments:
- tokens: bfloat16 [4, 8192, 768], P('wt', 'seq'), may hold values from -6 to 6
- in_w: float32 [2, 768, 3352], P(None, 'wt'), may hold values from -0.21875 to 0.21875
- in_m: float32 [2, 768, 3352], P(None, 'wt'), may hold values from -64 to 64
- in_v: float32 [2, 768, 3352], P(None, 'wt'), may hold values from 218.56256 to 3276.8
- out_w: float32 [2, 1536, 768], P(None, 'wt'), may hold values from -0.15625 to 0.15625
- out_m: float32 [2, 1536, 768], P(None, 'wt'), may hold values from -64 to 64
- out_v: float32 [2, 1536, 768], P(None, 'wt'), may hold values from 218.56256 to 3276.8
- small_params: float32 [2, 11336], P(None, 'wt'), as said below
- small_m: float32 [2, 11336], P(None, 'wt'), may hold values from -64 to 64
- small_v: float32 [2, 11336], P(None, 'wt'), may hold values from 218.56256 to 3276.8
- cotangent: bfloat16 [4, 8192, 768], P('wt', 'seq'), may hold values from -6 to 6
Outputs:
- layer_out: float32 [4, 8192, 768], P('wt', 'seq')
- input_grad: float32 [4, 8192, 768], P('wt', 'seq')
- new_in_m: float32 [2, 768, 3352], P(None, 'wt')
- new_in_v: float32 [2, 768, 3352], P(None, 'wt')
- new_in_w: float32 [2, 768, 3352], P(None, 'wt')
- new_out_m: float32 [2, 1536, 768], P(None, 'wt')
- new_out_v: float32 [2, 1536, 768], P(None, 'wt')
- new_out_w: float32 [2, 1536, 768], P(None, 'wt')
- new_small_m: float32 [2, 11336], P(None, 'wt')
- new_small_v: float32 [2, 11336], P(None, 'wt')
- new_small: float32 [2, 11336], P(None, 'wt')
Inputs may be any that keep to these rules, and one draw needn't show every extreme that they name: `small_params`: each row is one layer: gains near one, convolution taps of both signs, decay logarithms between log(1.6 / 8192) and log(0.17), step biases between -1.5 and -0.5, skip gains between 0.5 and 1.5.
All inputs are finite; a program needn't handle non-finite values.
Results may differ from a plain program's by a relative error of at most 0.019.
The roundings to bfloat16 on the way count: a program that leaves them out, or rounds other values in their place, can miss the bound.
Values may be sent and summed in bfloat16 or wider, within the bound.
No kernel may reach another device: no remote copies, remote signals or barrier semaphores. Data moves between devices by JAX's collectives and lax.ppermute only.
A program may use at most 320 MiB of HBM per device.

v0:
```python
import math

import jax
import jax.numpy as jnp
from jax import lax
from jax.sharding import PartitionSpec as P

D = 768
HEADS = 24
HDIM = 64
NSTATE = 128
WIDTH = 4
STEP = 10
INNER = 1536
CONV = 1792


highest = lax.Precision.HIGHEST


def passed_along(block, axis, distance):
    devices = range(lax.axis_size(axis))
    route = [(i - distance, i) for i in devices if i - distance in devices]
    return lax.ppermute(block, axis, route)


def entering(value, axis, join, neutral):
    count, mine = (lax.axis_size(axis), lax.axis_index(axis))
    pieces = jax.tree.map(lambda part: lax.all_gather(part, axis), value)
    subtotal = jax.tree.map(
        lambda part, zero: jnp.full_like(part, 0) + jnp.asarray(zero, part.dtype), value, neutral
    )

    def step(position, subtotal):
        longer = join(subtotal, jax.tree.map(lambda part: part[position], pieces))
        return jax.tree.map(lambda new, old: jnp.where(position < mine, new, old), longer, subtotal)

    return lax.fori_loop(0, count - 1, step, subtotal)


def entering_2(array, axis, combine, identity):
    peers, mine = (lax.axis_size(axis), lax.axis_index(axis))
    everything = jax.tree.map(
        lambda part, kind: lax.all_gather(part.astype(kind), axis),
        array,
        (jnp.bfloat16, jnp.bfloat16),
    )
    start = jax.tree.map(
        lambda part, zero: jnp.broadcast_to(jnp.asarray(zero, part.dtype), part.shape),
        array,
        identity,
    )

    def step(k, before):
        reached = k < mine
        new = combine(
            before, jax.tree.map(lambda part, own: part[k].astype(own.dtype), everything, array)
        )
        return jax.tree.map(lambda a, b: jnp.where(reached, a, b), new, before)

    return lax.fori_loop(0, peers, step, start)


def entering_3(array, axis, join, neutral):
    count = lax.axis_size(axis)
    place = lax.axis_index(axis)
    ahead = count - 1 - place
    gathered = jax.tree.map(
        lambda a, kind: lax.all_gather(a.astype(kind), axis),
        array,
        jax.tree.map(lambda a: jnp.bfloat16 if a.dtype == jnp.float32 else a.dtype, array),
    )
    state = jax.tree.map(lambda a, e: jnp.zeros_like(a) + jnp.asarray(e, a.dtype), array, neutral)

    def one(step, state):
        source = count - 1 - step
        return join(
            state,
            jax.tree.map(
                lambda a, own: lax.dynamic_index_in_dim(a, source, 0, False).astype(own.dtype),
                gathered,
                array,
            ),
        )

    return lax.fori_loop(0, ahead, one, state)


def rms_scale(values, gain_values):
    return (
        values * lax.rsqrt(jnp.mean(values * values, axis=-1, keepdims=True) + 1e-05) * gain_values
    )


def split_params(params):
    gain_in = params[0:D]
    gain_out = params[D : D + INNER]
    offset = D + INNER
    conv_taps = params[offset : offset + WIDTH * CONV].reshape(WIDTH, CONV)
    offset = offset + WIDTH * CONV
    conv_bias = params[offset : offset + CONV]
    offset = offset + CONV
    decay_log = params[offset : offset + HEADS]
    dt_bias = params[offset + HEADS : offset + 2 * HEADS]
    skip_gain = params[offset + 2 * HEADS : offset + 3 * HEADS]
    return (gain_in, gain_out, conv_taps, conv_bias, decay_log, dt_bias, skip_gain)


def prepare(projected, edge_rows, params):
    param_parts = split_params(params)
    conv_taps = param_parts[2]
    row_count = projected.shape[0]
    z_part = projected[:, :INNER]
    conv_in = projected[:, INNER : INNER + CONV]
    dt_raw = projected[:, INNER + CONV :]
    padded = jnp.concatenate([edge_rows, conv_in], axis=0)
    conv_sum = param_parts[3][None, :] + conv_taps[0][None, :] * padded[0:row_count]
    for offset in range(1, WIDTH):
        conv_sum = conv_sum + conv_taps[offset][None, :] * padded[offset : offset + row_count]
    conv_out = jax.nn.silu(conv_sum)
    x_heads = conv_out[:, :INNER].reshape(row_count, HEADS, HDIM)
    b_proj = conv_out[:, INNER : INNER + NSTATE]
    c_proj = conv_out[:, INNER + NSTATE :]
    step_size = jax.nn.softplus(dt_raw + param_parts[5][None, :])
    log_decay = -step_size * jnp.exp(param_parts[4])[None, :]
    return (z_part, x_heads, b_proj, c_proj, log_decay, step_size)


def scan_blocks(x_heads, b_proj, c_proj, log_decay, step_size, block_rows):
    row_count = x_heads.shape[0]
    block_count = row_count // block_rows
    pieces = (
        x_heads.reshape(block_count, block_rows, HEADS, HDIM),
        b_proj.reshape(block_count, block_rows, NSTATE),
        c_proj.reshape(block_count, block_rows, NSTATE),
        log_decay.reshape(block_count, block_rows, HEADS),
        step_size.reshape(block_count, block_rows, HEADS),
    )
    causal = jnp.arange(block_rows)[:, None] >= jnp.arange(block_rows)[None, :]

    def one_block(states, piece_set):
        heads_block, b_block, c_block, decay_block, step_block = piece_set
        cum_decay = jnp.cumsum(decay_block, axis=0)
        cum_heads = cum_decay.T
        pair_diff = cum_heads[:, :, None] - cum_heads[:, None, :]
        decay_pairs = jnp.exp(jnp.where(causal[None], pair_diff, -1e30))
        scores = jnp.dot(c_block, b_block.T, precision=highest)
        weight_mat = decay_pairs * scores[None] * step_block.T[:, None, :]
        within = jnp.einsum("hij,jhp->ihp", weight_mat, heads_block, precision=highest)
        carried = (
            jnp.einsum("in,hpn->ihp", c_block, states, precision=highest)
            * jnp.exp(cum_decay)[:, :, None]
        )
        tail_weight = jnp.exp(cum_decay[-1:] - cum_decay) * step_block
        new_states = jnp.exp(cum_decay[-1])[:, None, None] * states + jnp.einsum(
            "jh,jhp,jn->hpn", tail_weight, heads_block, b_block, precision=highest
        )
        return (new_states, within + carried)

    final_states, outputs = lax.scan(
        jax.checkpoint(one_block), jnp.zeros((HEADS, HDIM, NSTATE), jnp.float32), pieces
    )
    return (outputs.reshape(row_count, HEADS, HDIM), final_states)


def gate_out(ssm_heads, z_part, x_heads, params):
    param_parts = split_params(params)
    with_skip = ssm_heads + param_parts[6][None, :, None] * x_heads
    flat_out = with_skip.reshape(z_part.shape[0], INNER)
    return rms_scale(flat_out * jax.nn.silu(z_part), param_parts[1])


def inject(ssm_local, z_part, x_heads, c_proj, log_decay, states_in, params):
    cum_all = jnp.cumsum(log_decay, axis=0)
    carried = (
        jnp.einsum("tn,hpn->thp", c_proj, states_in, precision=highest)
        * jnp.exp(cum_all)[:, :, None]
    )
    return gate_out(ssm_local + carried, z_part, x_heads, params)


def chain_step(earlier, later):
    return (earlier[0] * later[0], later[0][:, None, None] * earlier[1] + later[1])


def norm_in(rows_in, vec_in):
    return rms_scale(rows_in, vec_in[:D])


def mix_forward(hidden_rows, in_weight, out_weight, params, send_edge, pass_states):
    row_count = hidden_rows.shape[0]
    block_rows = math.gcd(row_count, 256)
    normed, norm_back = jax.vjp(norm_in, hidden_rows, params)
    normed_low = normed.astype(jnp.bfloat16)
    projected = jnp.dot(normed_low, in_weight, preferred_element_type=jnp.float32)
    edge_rows = send_edge(projected[row_count - WIDTH + 1 :, INNER : INNER + CONV])
    prepared, prep_back = jax.vjp(prepare, projected, edge_rows, params)
    z_part, x_heads, b_proj, c_proj, log_decay, step_size = prepared

    def run_blocks(heads_in, b_in, c_in, decay_in, step_in):
        return scan_blocks(heads_in, b_in, c_in, decay_in, step_in, block_rows)

    core_out, core_back = jax.vjp(run_blocks, x_heads, b_proj, c_proj, log_decay, step_size)
    ssm_local, local_states = core_out
    total_decay = jnp.exp(jnp.sum(log_decay, axis=0))
    states_in = pass_states(total_decay, local_states)
    gated, gate_back = jax.vjp(
        inject, ssm_local, z_part, x_heads, c_proj, log_decay, states_in, params
    )
    gated_low = gated.astype(jnp.bfloat16)
    branch = jnp.dot(gated_low, out_weight, preferred_element_type=jnp.float32)
    kept_state = (
        norm_back,
        normed_low,
        prep_back,
        core_back,
        gate_back,
        total_decay,
        states_in,
        gated_low,
    )
    return (hidden_rows + branch, kept_state)


def mix_backward(grad_rows, in_weight, out_weight, kept_state, return_states, return_edge):
    norm_back, normed_low, prep_back, core_back, gate_back, total_decay, states_in, gated_low = (
        kept_state
    )
    grad_low = grad_rows.astype(jnp.bfloat16)
    out_grad = jnp.dot(gated_low.T, grad_low, preferred_element_type=jnp.float32)
    gated_grad = jnp.dot(grad_low, out_weight.T, preferred_element_type=jnp.float32)
    ssm_grad, z_grad, heads_grad, c_grad, decay_grad, local_grad, params_grad = gate_back(
        gated_grad
    )
    later_grad = return_states(total_decay, local_grad)
    total_grad = jnp.sum(later_grad * states_in, axis=(1, 2)) * total_decay
    heads_more, b_grad, c_more, decay_more, step_grad = core_back((ssm_grad, later_grad))
    projected_grad, edge_grad, params_more = prep_back(
        (
            z_grad,
            heads_grad + heads_more,
            b_grad,
            c_grad + c_more,
            decay_grad + decay_more + total_grad[None, :],
            step_grad,
        )
    )
    from_next = return_edge(edge_grad)
    row_count = projected_grad.shape[0]
    projected_grad = projected_grad.at[row_count - WIDTH + 1 :, INNER : INNER + CONV].add(from_next)
    projected_low = projected_grad.astype(jnp.bfloat16)
    in_grad = jnp.dot(normed_low.T, projected_low, preferred_element_type=jnp.float32)
    normed_grad = jnp.dot(projected_low, in_weight.T, preferred_element_type=jnp.float32)
    rows_grad, params_norm = norm_back(normed_grad)
    return (grad_rows + rows_grad, in_grad, out_grad, params_grad + params_more + params_norm)


def adam_step(weight, moment, second, gradient, learn_rate, weight_decay):
    new_moment = 0.9 * moment + 0.1 * gradient
    new_second = 0.95 * second + 0.05 * gradient * gradient
    corrected = new_moment / (1.0 - 0.9**STEP) / (jnp.sqrt(new_second / (1.0 - 0.95**STEP)) + 1e-08)
    return (new_moment, new_second, weight - learn_rate * (corrected + weight_decay * weight))


def shards(
    tokens, in_w, in_m, in_v, out_w, out_m, out_v, small_params, small_m, small_v, cotangent
):
    layer_count = in_w.shape[0]
    in_full, out_full, small_full = (
        lax.all_gather(in_w.astype(jnp.bfloat16), "wt", axis=1, tiled=True),
        lax.all_gather(out_w.astype(jnp.bfloat16), "wt", axis=1, tiled=True),
        lax.all_gather(small_params.astype(jnp.bfloat16), "wt", axis=1, tiled=True),
    )

    def send_edge(edge_rows):
        return passed_along(edge_rows, "seq", 1)

    def pass_states(total_decay, local_states):
        return entering(
            (total_decay, local_states),
            "seq",
            chain_step,
            (jnp.ones_like(total_decay), jnp.zeros_like(local_states)),
        )[1]

    hidden_rows = tokens[0].astype(jnp.float32)
    layer_inputs = []
    saved_all = []
    for layer_index in range(layer_count):
        layer_inputs.append(hidden_rows)
        hidden_rows, kept_state = mix_forward(
            hidden_rows,
            in_full[layer_index],
            out_full[layer_index],
            small_full[layer_index].astype(jnp.float32),
            send_edge,
            pass_states,
        )
        saved_all.append(kept_state)
    in_back, out_back, small_back = (
        lax.all_gather(in_w.astype(jnp.bfloat16), "wt", axis=1, tiled=True),
        lax.all_gather(out_w.astype(jnp.bfloat16), "wt", axis=1, tiled=True),
        lax.all_gather(small_params.astype(jnp.bfloat16), "wt", axis=1, tiled=True),
    )

    def send_again(edge_rows):
        return passed_along(edge_rows, "seq", 1)

    def pass_again(total_decay, local_states):
        return entering_2(
            (total_decay, local_states),
            "seq",
            chain_step,
            (jnp.ones_like(total_decay), jnp.zeros_like(local_states)),
        )[1]

    def return_states(total_decay, local_grad):
        return entering_3(
            (total_decay, local_grad),
            "seq",
            chain_step,
            (jnp.ones_like(total_decay), jnp.zeros_like(local_grad)),
        )[1]

    def return_edge(edge_grad):
        return passed_along(edge_grad, "seq", -1)

    grad_rows = cotangent[0].astype(jnp.float32)
    in_grads = [None] * layer_count
    out_grads = [None] * layer_count
    small_grads = [None] * layer_count
    for layer_index in reversed(range(layer_count)):
        redone = mix_forward(
            layer_inputs[layer_index],
            in_back[layer_index],
            out_back[layer_index],
            small_back[layer_index].astype(jnp.float32),
            send_again,
            pass_again,
        )
        kept_state = redone[1]
        grad_rows, in_grads[layer_index], out_grads[layer_index], small_grads[layer_index] = (
            mix_backward(
                grad_rows,
                in_back[layer_index],
                out_back[layer_index],
                kept_state,
                return_states,
                return_edge,
            )
        )
    in_stack = jnp.stack(in_grads)
    out_stack = jnp.stack(out_grads)
    small_stack = jnp.stack(small_grads)
    seq_count = lax.axis_size("seq")
    wt_count = lax.axis_size("wt")

    def regroup(full_grad):
        shape_in = full_grad.shape
        split_view = full_grad.reshape(
            shape_in[0], wt_count, seq_count, shape_in[1] // (wt_count * seq_count), shape_in[2]
        )
        return jnp.swapaxes(split_view, 1, 2).reshape(shape_in)

    in_part, out_part = (
        lax.psum_scatter(regroup(in_stack), ("seq", "wt"), scatter_dimension=1, tiled=True),
        lax.psum_scatter(regroup(out_stack), ("seq", "wt"), scatter_dimension=1, tiled=True),
    )
    small_total_all = lax.psum(small_stack, ("seq", "wt"))
    in_total, out_total = (
        lax.all_gather(in_part.astype(jnp.bfloat16), "seq", axis=1, tiled=True).astype(
            in_part.dtype
        ),
        lax.all_gather(out_part.astype(jnp.bfloat16), "seq", axis=1, tiled=True).astype(
            out_part.dtype
        ),
    )
    shard_width = small_total_all.shape[1] // wt_count
    small_total = lax.dynamic_slice_in_dim(
        small_total_all, lax.axis_index("wt") * shard_width, shard_width, 1
    )
    new_in_m, new_in_v, new_in_w = adam_step(in_w, in_m, in_v, in_total, 0.03, 0.1)
    new_out_m, new_out_v, new_out_w = adam_step(out_w, out_m, out_v, out_total, 0.02, 0.1)
    new_small_m, new_small_v, new_small = adam_step(
        small_params, small_m, small_v, small_total, 0.2, 0.0
    )
    return (
        hidden_rows[None],
        grad_rows[None],
        new_in_m,
        new_in_v,
        new_in_w,
        new_out_m,
        new_out_v,
        new_out_w,
        new_small_m,
        new_small_v,
        new_small,
    )


def solution(mesh):
    return jax.shard_map(
        shards,
        mesh=mesh,
        in_specs=(
            P("wt", "seq", None),
            P(None, "wt", None),
            P(None, "wt", None),
            P(None, "wt", None),
            P(None, "wt", None),
            P(None, "wt", None),
            P(None, "wt", None),
            P(None, "wt"),
            P(None, "wt"),
            P(None, "wt"),
            P("wt", "seq", None),
        ),
        out_specs=(
            P("wt", "seq", None),
            P("wt", "seq", None),
            P(None, "wt", None),
            P(None, "wt", None),
            P(None, "wt", None),
            P(None, "wt", None),
            P(None, "wt", None),
            P(None, "wt", None),
            P(None, "wt"),
            P(None, "wt"),
            P(None, "wt"),
        ),
        check_vma=False,
    )
```

profile of v0, /device:TPU:1, one launch (start us, length us, event | category | flops | bytes accessed | tf_op | source)
XLA Modules:
  0.0 1393.2 jit_solution(16303373069124025850)
XLA Ops:
  7.2 4.3 convert_element_type.224
  12.2 10.4 all-gather.10
  24.4 92.5 %all-gather.22.cloned.1.call-done = bf16[2,768,3352]{2,1,0:T(8,128)(2,1)} async-done(((bf16[2,192,3352]{2,1,0:T(8,128)(2,1)}), bf16[2,768,3352]{2,1,0:T(8,128)(2,1)}) %all-gather.22.cloned.1.call-update) | async-done | bytes 10297360 | tf_op jit(solution)/shard_map/all_gather | solution.py:270
  116.9 4.8 fusion.27
  137.1 7.8 fusion.73
  154.9 62.6 %all-reduce.46 = f32[768]{0:T(1024)S(1)} all-reduce(f32[768]{0:T(1024)S(1)} %get-tuple-element.1138), channel_id=2, replica_groups=mesh['seq'=32,'wt'=4] {'seq'}, use_global_device_ids=true, to_apply=%add.46 | all-reduce | flops 768 | bytes 6144
  221.3 8.3 bitcast_add_fusion.7
  229.7 11.9 all-gather.30.cloned.1.call-done
  241.5 42.0 %while.58 = (s32[]{:T(128)}, f32[24,64,128]{2,1,0:T(8,128)S(1)}, s32[]{:T(128)}, f32[32,24]{1,0:T(8,128)S(1)}, f32[32,24,64,128]{3,2,1,0:T(8,128)}, /*index=5*/s32[]{:T(128)}, s32[]{:T(128)}) while((s32[]{:T(128)}, f32[24,64,128]{2,1,0:T(8,128)S(1)}, s32[]{:T(128)}, f32[32,24]{1,0:T(8,128)S(1)}, f32[32,24,64,128]{3,2,1,0:T(8,128)}, ...), condition=%wide.region_5.6_spmd.clone, body=%wide.region_4.5_spmd.clone.sunk | while | flops 786436 | bytes 2359689 | solution.py:38
  288.8 6.4 all-gather.24.cloned.1.call-done
  298.5 4.8 fusion.29
  313.9 7.6 fusion.72
  327.7 62.2 %all-reduce.47 = f32[768]{0:T(1024)S(1)} all-reduce(f32[768]{0:T(1024)S(1)} %get-tuple-element.1140), channel_id=4, replica_groups=mesh['seq'=32,'wt'=4] {'seq'}, use_global_device_ids=true, to_apply=%add.47 | all-reduce | flops 768 | bytes 6144
  390.2 67.6 %all-reduce.53 = (bf16[768]{0:T(1024)(128)(2,1)S(1)}, bf16[768]{0:T(1024)(128)(2,1)S(1)}) all-reduce(bf16[768]{0:T(1024)(128)(2,1)S(1)} %dynamic-update-slice.6, bf16[768]{0:T(1024)(128)(2,1)S(1)} %dynamic-update-slice.7), channel_id=6, replica_groups=mesh['seq'=32,'wt'=4] {'seq'}, use_global_device_ids=true, to_apply=%add.48 | all-reduce | flops 1536 | bytes 6144
  462.8 39.3 %while.60 = (s32[]{:T(128)}, f32[24,64,128]{2,1,0:T(8,128)S(1)}, s32[]{:T(128)}, bf16[32,24]{1,0:T(8,128)(2,1)S(1)}, bf16[32,24,64,128]{3,2,1,0:T(8,128)(2,1)}, /*index=5*/s32[]{:T(128)}, s32[]{:T(128)}) while((s32[]{:T(128)}, f32[24,64,128]{2,1,0:T(8,128)S(1)}, s32[]{:T(128)}, bf16[32,24]{1,0:T(8,128)(2,1)S(1)}, ...), condition=%wide.region_18.20_spmd.clone, body=%wide.region_17.19_spmd.clone.sunk | while | flops 983068 | bytes 1966425 | solution.py:61
  504.8 10.0 add_add_fusion.3
  520.2 75.6 %while.59 = (s32[]{:T(128)}, f32[24,64,128]{2,1,0:T(8,128)}, s32[]{:T(128)}, f32[32,24]{1,0:T(8,128)S(1)}, f32[32,24,64,128]{3,2,1,0:T(8,128)}, /*index=5*/s32[]{:T(128)}, s32[]{:T(128)}) while((s32[]{:T(128)}, f32[24,64,128]{2,1,0:T(8,128)}, s32[]{:T(128)}, f32[32,24]{1,0:T(8,128)S(1)}, f32[32,24,64,128]{3,2,1,0:T(8,128)}, ...), condition=%wide.region_12.13_spmd.clone, body=%wide.region_11.12_spmd.clone.sunk | while | flops 786436 | bytes 2359689 | solution.py:38
  599.3 5.2 multiply_reduce_fusion.15
  607.8 74.0 %while.61 = (s32[]{:T(128)}, f32[24,64,128]{2,1,0:T(8,128)}, s32[]{:T(128)}, bf16[32,24]{1,0:T(8,128)(2,1)S(1)}, bf16[32,24,64,128]{3,2,1,0:T(8,128)(2,1)}, /*index=5*/s32[]{:T(128)}, s32[]{:T(128)}) while((s32[]{:T(128)}, f32[24,64,128]{2,1,0:T(8,128)}, s32[]{:T(128)}, bf16[32,24]{1,0:T(8,128)(2,1)S(1)}, ...), condition=%wide.region_43.45_spmd.clone, body=%wide.region_42.44_spmd.clone.sunk | while | flops 983068 | bytes 1966425 | solution.py:61
  681.8 4.4 add_add_fusion.2
  697.5 57.6 %while.56 = (s32[]{:T(128)}, f32[24,64,128]{2,1,0:T(8,128)S(1)}, s32[]{:T(128)}, bf16[32,24]{1,0:T(8,128)(2,1)}, bf16[32,24,64,128]{3,2,1,0:T(8,128)(2,1)}, /*index=5*/s32[]{:T(128)}, s32[]{:T(128)}, s32[]{:T(128)}, s32[]{:T(128)}) while((s32[]{:T(128)}, f32[24,64,128]{2,1,0:T(8,128)S(1)}, s32[]{:T(128)}, bf16[32,24]{1,0:T(8,128)(2,1)}, ...), condition=%wide.region_22.24_spmd, body=%wide.region_21.23_spmd.sunk | while | flops 589854 | bytes 1966467 | solution.py:86
  766.7 10.4 fusion.31
  789.8 5.4 bitcast_add_fusion.5
  798.2 4.0 multiply_reduce_fusion.6
  809.1 4.6 collective-permute-start.2
  818.2 6.3 scatter-add.6
  824.5 6.0 multiply_reduce_fusion.28
  844.9 4.5 convolution_bitcast_fusion.1
  858.5 4.4 fusion.174
  863.0 6.4 stack.25
  869.4 5.5 copy.384
  878.7 8.6 copy.385
  887.3 5.7 fusion.162
  893.0 13.0 stack.23
  906.0 11.0 copy.380
  919.8 57.4 %while.57 = (s32[]{:T(128)}, f32[24,64,128]{2,1,0:T(8,128)S(1)}, s32[]{:T(128)}, bf16[32,24]{1,0:T(8,128)(2,1)}, bf16[32,24,64,128]{3,2,1,0:T(8,128)(2,1)}, /*index=5*/s32[]{:T(128)}, s32[]{:T(128)}, s32[]{:T(128)}, s32[]{:T(128)}) while((s32[]{:T(128)}, f32[24,64,128]{2,1,0:T(8,128)S(1)}, s32[]{:T(128)}, bf16[32,24]{1,0:T(8,128)(2,1)}, ...), condition=%wide.region_47.49_spmd, body=%wide.region_46.48_spmd.sunk | while | flops 589854 | bytes 1966467 | solution.py:86
  980.4 4.0 multiply_reduce_fusion.12
  986.6 10.4 fusion.33
  1005.6 5.4 bitcast_add_fusion.3
  1035.4 8.4 scatter-add.9
  1043.8 4.2 fusion.26
  1056.5 12.4 maximum_bitcast_fusion
  1068.9 37.1 %copy.381 = f32[2,32,4,6,3352]{4,0,3,2,1:T(2,128)} copy(f32[2,32,4,6,3352]{4,1,3,2,0:T(8,128)} %maximum_bitcast_fusion) | data formatting | bytes 41189376 | tf_op jit(solution)/shard_map/transpose | solution.py:363
  1106.1 178.6 %all-reduce.58 = (bf16[2,768,3352]{2,0,1:T(2,128)(2,1)}, bf16[2,1536,768]{2,0,1:T(2,128)(2,1)}) all-reduce(f32[2,768,3352]{2,0,1:T(2,128)} %bitcast.590, f32[2,1536,768]{2,0,1:T(2,128)} %bitcast.618), channel_id=12, replica_groups=mesh['seq'=32,'wt'=4] {'seq','wt'}, use_global_device_ids=true, to_apply=%region_64.66.clone | all-reduce | flops 7507968 | bytes 45047808
  1294.2 33.6 %all-gather.28.cloned.1.call-done = bf16[2,384,768]{2,0,1:T(2,128)(2,1)} async-done(((bf16[2,12,768]{2,0,1:T(2,128)(2,1)}), bf16[2,384,768]{2,0,1:T(2,128)(2,1)}) %all-gather.28.cloned.1.call-update) | async-done | bytes 1179664 | tf_op jit(solution)/shard_map/all_gather | solution.py:374
  1327.9 6.9 multiply_subtract_fusion.1
  1334.7 40.2 %all-gather.26.cloned.1.call-done = bf16[2,192,3352]{2,0,1:T(2,128)(2,1)} async-done(((bf16[2,6,3352]{2,0,1:T(2,128)(2,1)}), bf16[2,192,3352]{2,0,1:T(2,128)(2,1)}) %all-gather.26.cloned.1.call-update) | async-done | bytes 2574352 | tf_op jit(solution)/shard_map/all_gather | solution.py:371
  1374.9 11.5 multiply_subtract_fusion
  (970 shorter events, 552.6 us)
Async XLA Ops:
  7.2 109.7 %all-gather.22.cloned.1.call-start = ((), (), s32[]{:S(2)}) async-start(), calls=%async_computation | async-start | bytes 13271040 | tf_op jit(solution)/shard_map/all_gather | solution.py:270
  11.5 230.0 %all-gather.30.cloned.1.call-start = ((), (), s32[]{:S(2)}) async-start(), calls=%async_computation.5 | async-start | bytes 25952256 | tf_op jit(solution)/shard_map/all_gather | solution.py:29
  22.9 94.0 %copy-start.79 = (f32[1,11336]{1,0:T(1,128)}, f32[1,11336]{1,0:T(1,128)S(1)}, u32[]{:S(2)}) copy-start(f32[1,11336]{1,0:T(1,128)S(1)} %get-tuple-element.1115) | copy-start | bytes 136036
  22.9 94.0 %copy-start.80 = (f32[1,11336]{1,0:T(1,128)}, f32[1,11336]{1,0:T(1,128)S(1)}, u32[]{:S(2)}) copy-start(f32[1,11336]{1,0:T(1,128)S(1)} %get-tuple-element.1114) | copy-start | bytes 136036
  22.9 98.8 %copy-start.110 = (f32[768]{0:T(1024)}, f32[768]{0:T(1024)S(1)}, u32[]{:S(2)}) copy-start(f32[768]{0:T(1024)S(1)} %get-tuple-element.1159) | copy-start | bytes 9220
  22.9 275.6 %copy-start.77 = (f32[768]{0:T(1024)}, f32[768]{0:T(1024)S(1)}, u32[]{:S(2)}) copy-start(f32[768]{0:T(1024)S(1)} %get-tuple-element.1158) | copy-start | bytes 9220
  23.6 113.4 %copy-start.90 = (f32[1792]{0:T(1024)}, f32[1792]{0:T(1024)S(1)}, u32[]{:S(2)}) copy-start(f32[1792]{0:T(1024)S(1)} %get-tuple-element.982) | copy-start | bytes 21508
  23.6 113.4 %copy-start.92 = (f32[1792]{0:T(1024)}, f32[1792]{0:T(1024)S(1)}, u32[]{:S(2)}) copy-start(f32[1792]{0:T(1024)S(1)} %get-tuple-element.983) | copy-start | bytes 21508
  23.8 93.1 %copy-start.136 = (f32[256]{0:T(256)}, f32[256]{0:T(256)S(1)}, u32[]{:S(2)}) copy-start(f32[256]{0:T(256)S(1)} %fusion.167) | copy-start | bytes 3076
  24.4 98.9 %copy-start.151 = (f32[24]{0:T(128)}, f32[24]{0:T(128)S(1)}, u32[]{:S(2)}) copy-start(f32[24]{0:T(128)S(1)} %get-tuple-element.1117) | copy-start | bytes 292
  24.4 98.9 %copy-start.152 = (f32[24]{0:T(128)}, f32[24]{0:T(128)S(1)}, u32[]{:S(2)}) copy-start(f32[24]{0:T(128)S(1)} %get-tuple-element.1118) | copy-start | bytes 292
  24.4 97.3 %copy-start.133 = (f32[256]{0:T(256)}, f32[256]{0:T(256)S(1)}, u32[]{:S(2)}) copy-start(f32[256]{0:T(256)S(1)} %fusion.244) | copy-start | bytes 3076
  124.1 97.2 %copy-start.61 = (f32[256,24]{0,1:T(8,128)}, f32[256,24]{0,1:T(8,128)S(1)}, u32[]{:S(2)}) copy-start(f32[256,24]{0,1:T(8,128)S(1)} %get-tuple-element.843) | copy-start | bytes 73732
  128.9 7.0 collective-permute-start
  133.4 150.1 %copy-start.65 = (f32[256,24]{0,1:T(8,128)}, f32[256,24]{0,1:T(8,128)S(1)}, u32[]{:S(2)}) copy-start(f32[256,24]{0,1:T(8,128)S(1)} %get-tuple-element.1134) | copy-start | bytes 73732
  145.0 536.7 %copy-start = (f32[256,1536]{0,1:T(8,128)}, f32[256,1536]{0,1:T(8,128)S(1)}, u32[]{:S(2)}) copy-start(f32[256,1536]{0,1:T(8,128)S(1)} %slice.514) | copy-start | bytes 4718596
  148.1 147.1 %all-gather.24.cloned.1.call-start = ((), (), s32[]{:S(2)}) async-start(), calls=%async_computation.1 | async-start | bytes 5898240 | tf_op jit(solution)/shard_map/all_gather | solution.py:271
  150.9 70.4 %copy-start.122 = (f32[24,256]{1,0:T(8,128)S(1)}, f32[24,256]{1,0:T(8,128)}, u32[]{:S(2)}) copy-start(f32[24,256]{1,0:T(8,128)} %get-tuple-element.1136) | copy-start | bytes 73732
  150.9 311.8 %all-gather.34.cloned.1.call-start = ((), (), s32[]{:S(2)}) async-start(), calls=%async_computation.7 | async-start | bytes 12976128 | tf_op jit(solution)/shard_map/all_gather | solution.py:44
  151.0 78.6 %copy-start.104 = (pred[256,256]{1,0:T(8,128)(4,1)}, pred[256,256]{1,0:T(8,128)(4,1)S(1)}, u32[]{:S(2)}) copy-start(pred[256,256]{1,0:T(8,128)(4,1)S(1)} %iota_compare_fusion) | copy-start | bytes 196612
  151.8 143.4 %copy-start.75 = (f32[1536]{0:T(1024)}, f32[1536]{0:T(1024)S(1)}, u32[]{:S(2)}) copy-start(f32[1536]{0:T(1024)S(1)} %slice_reduce_fusion.23) | copy-start | bytes 18436
  241.5 42.0 %copy-start.145 = (f32[24]{0:T(128)S(1)}, f32[24]{0:T(128)}, u32[]{:S(2)}) copy-start(f32[24]{0:T(128)} %get-tuple-element.1116) | copy-start | bytes 292
  305.3 22.2 %copy-start.160 = (f32[24]{0:T(128)}, f32[24]{0:T(128)S(1)}, u32[]{:S(2)}) copy-start(f32[24]{0:T(128)S(1)} %get-tuple-element.1073) | copy-start | bytes 292
  306.7 6.8 collective-permute-start.1
  325.8 194.4 %all-gather.32.cloned.1.call-start = ((), (), s32[]{:S(2)}) async-start(), calls=%async_computation.6 | async-start | bytes 25952256 | tf_op jit(solution)/shard_map/all_gather | solution.py:29
  326.4 281.4 %all-gather.38.cloned.1.call-start = ((), (), s32[]{:S(2)}) async-start(), calls=%async_computation.9 | async-start | bytes 12976128 | tf_op jit(solution)/shard_map/all_gather | solution.py:44
  327.2 272.1 %copy-start.83 = (f32[1536]{0:T(1024)}, f32[1536]{0:T(1024)S(1)}, u32[]{:S(2)}) copy-start(f32[1536]{0:T(1024)S(1)} %slice_reduce_fusion.22) | copy-start | bytes 18436
  327.5 370.0 %all-gather.36.cloned.1.call-start = ((), (), s32[]{:S(2)}) async-start(), calls=%async_computation.8 | async-start | bytes 12976128 | tf_op jit(solution)/shard_map/all_gather | solution.py:69
  520.2 75.6 %copy-start.8 = (f32[256,1536]{0,1:T(8,128)S(1)}, f32[256,1536]{0,1:T(8,128)}, u32[]{:S(2)}) copy-start(f32[256,1536]{0,1:T(8,128)} %copy-done.6) | copy-start | bytes 4718596
  606.7 313.0 %all-gather.40.cloned.1.call-start = ((), (), s32[]{:S(2)}) async-start(), calls=%async_computation.10 | async-start | bytes 12976128 | tf_op jit(solution)/shard_map/all_gather | solution.py:69
  607.8 74.0 %copy-start.66 = (f32[256,24]{0,1:T(8,128)S(1)}, f32[256,24]{0,1:T(8,128)}, u32[]{:S(2)}) copy-start(f32[256,24]{0,1:T(8,128)} %copy-done.65) | copy-start | bytes 73732
  607.8 74.0 %copy-start.146 = (f32[24]{0:T(128)S(1)}, f32[24]{0:T(128)}, u32[]{:S(2)}) copy-start(f32[24]{0:T(128)} %get-tuple-element.1116) | copy-start | bytes 292
  697.5 57.9 %copy-start.161 = (f32[24]{0:T(128)S(1)}, f32[24]{0:T(128)}, u32[]{:S(2)}) copy-start(f32[24]{0:T(128)} %copy-done.160) | copy-start | bytes 292
  756.0 30.5 %copy-start.11 = (f32[24,64,128]{2,1,0:T(8,128)}, f32[24,64,128]{2,1,0:T(8,128)S(1)}, u32[]{:S(2)}) copy-start(f32[24,64,128]{2,1,0:T(8,128)S(1)} %broadcast.423) | copy-start | bytes 2359300
  809.1 7.1 collective-permute-start.2
  830.8 27.7 %copy-start.38 = (f32[256,768]{1,0:T(8,128)}, f32[256,768]{1,0:T(8,128)S(1)}, u32[]{:S(2)}) copy-start(f32[256,768]{1,0:T(8,128)S(1)} %fusion.171) | copy-start | bytes 2359300
  840.2 452.5 %all-reduce.57.cloned.1.call-start = ((), (), s32[]{:S(2)}) async-start(), calls=%async_computation.4 | async-start | bytes 182272 | tf_op jit(solution)/shard_map/psum | solution.py:369
  919.8 57.7 %copy-start.159 = (f32[24]{0:T(128)S(1)}, f32[24]{0:T(128)}, u32[]{:S(2)}) copy-start(f32[24]{0:T(128)} %get-tuple-element.1078) | copy-start | bytes 292
  979.5 17.5 %copy-start.116 = (f32[24,2]{0,1:T(2,128)}, f32[24,2]{0,1:T(2,128)S(1)}, u32[]{:S(2)}) copy-start(f32[24,2]{0,1:T(2,128)S(1)} %slice.493) | copy-start | bytes 580
  980.4 16.6 %copy-start.142 = (f32[24]{0:T(128)}, f32[24]{0:T(128)S(1)}, u32[]{:S(2)}) copy-start(f32[24]{0:T(128)S(1)} %get-tuple-element.1122) | copy-start | bytes 292
  1025.3 5.6 collective-permute-start.3
  1050.0 277.9 %all-gather.28.cloned.1.call-start = ((), (), s32[]{:S(2)}) async-start(), calls=%async_computation.3 | async-start | bytes 1216512 | tf_op jit(solution)/shard_map/all_gather | solution.py:374
  1106.0 181.7 %copy-start.156 = (f32[256]{0:T(256)S(1)}, f32[256]{0:T(256)}, u32[]{:S(2)}) copy-start(f32[256]{0:T(256)} %get-tuple-element.1090) | copy-start | bytes 3076
  1106.0 181.7 %copy-start.20 = (f32[256,768]{1,0:T(8,128)S(1)}, f32[256,768]{1,0:T(8,128)}, u32[]{:S(2)}) copy-start(f32[256,768]{1,0:T(8,128)} %copy-done.18) | copy-start | bytes 2359300
  1106.0 181.7 %copy-start.44 = (f32[256,1536]{0,1:T(8,128)S(1)}, f32[256,1536]{0,1:T(8,128)}, u32[]{:S(2)}) copy-start(f32[256,1536]{0,1:T(8,128)} %get-tuple-element.1089) | copy-start | bytes 4718596
  1106.1 181.7 %copy-start.84 = (f32[1536]{0:T(1024)S(1)}, f32[1536]{0:T(1024)}, u32[]{:S(2)}) copy-start(f32[1536]{0:T(1024)} %copy-done.83) | copy-start | bytes 18436
  1286.1 88.8 %all-gather.26.cloned.1.call-start = ((), (), s32[]{:S(2)}) async-start(), calls=%async_computation.2 | async-start | bytes 2737152 | tf_op jit(solution)/shard_map/all_gather | solution.py:371
  1291.5 36.4 %copy-start.31 = (f32[2,384,768]{2,1,0:T(8,128)S(1)}, f32[2,384,768]{2,1,0:T(8,128)}, u32[]{:S(2)}) copy-start(f32[2,384,768]{2,1,0:T(8,128)} %param.32) | copy-start | bytes 7077892
  (138 other events, 629.3 us)
Sparse Core Ops, SparseCore 0:
  11.6 105.1 all-gather.21
  148.2 93.3 all-gather.29
  243.8 51.3 all-gather.23
  325.9 63.2 all-gather.33
  391.9 92.1 all-gather.31
  486.2 61.9 all-gather.37
  606.8 58.6 all-gather.35
  840.3 58.4 all-gather.39
  1050.1 134.3 all-reduce.56
  1286.2 41.6 all-gather.27
  1331.0 43.8 all-gather.25
where the time goes:
time: 1410 us; the launch traced here: 1390 us
  other arithmetic  485 us (34%)
  blocking collectives  381 us (27%)
  waiting for transfers between devices  186 us (13%)
  local copies, waits for them, and re-layouts  152 us (11%)
  matrix products  152 us (11%)
  between operations  17.2 us (1%)
  starting transfers between devices  16.2 us (1%)
    unnamed x4, blocking collectives  371 us
    select_n x62, other arithmetic, step(): jnp.where(position < mine, new, old)  116 us
    select_n x64, other arithmetic, step(): return jax.tree.map(lambda a, b: jnp.where(reached, a, b), new, before)  112 us
    all_gather x1, waiting for transfers between devices, shards(): lax.all_gather(in_w.astype(jnp.bfloat16), 'wt', axis=1, tiled=True)  92.5 us
    add x60, other arithmetic, chain_step(): later[0][:, None, None] * earlier[1] + later[1]  71.8 us
    dot_general x6, matrix products, one_block(): jnp.einsum('hij,jhp->ihp', weight_mat, heads_block, precision=highest)  50 us
    transpose x2, local copies, waits for them, and re-layouts, regroup(): return jnp.swapaxes(split_view, 1, 2).reshape(shape_in)  45.7 us
    convert_element_type x60, other arithmetic, one(): lax.dynamic_index_in_dim(a, source, 0, False).astype(own.dtype)  41.2 us
  transfers between devices with their start and end apart: 15, of which 6 were waited for; matrix products, arithmetic and copies ran while one was open for 34% of the time, Pallas kernels for 0%

commit v1 on v0

v1 whole, which is shorter than its diff:
```python
import functools

import jax
import jax.numpy as jnp
from jax import lax
from jax.experimental import pallas as pl
from jax.experimental.pallas import tpu as pltpu
from jax.sharding import Mesh
from jax.sharding import PartitionSpec as P

D = 768
HEADS = 24
HDIM = 64
NSTATE = 128
WIDTH = 4
STEP = 10
INNER = 1536
CONV = 1792
PROJ = 3352
VEC = 11336
ROWS = 256
EPS = 1e-05
PAIRS = HEADS // 2
LANES = 128
PLANE = ("x", "z", "core")

bf16 = jnp.bfloat16
f32 = jnp.float32
VMEM_BYTES = 48 * 1024 * 1024


def call(kernel, outs, scratch=(), grid=(), in_specs=None, out_specs=None, flops=0, moved=0, **kw):
    params = pltpu.CompilerParams(vmem_limit_bytes=VMEM_BYTES)
    extra = {}
    if in_specs is not None:
        extra["in_specs"] = in_specs
        extra["out_specs"] = out_specs
    return pl.pallas_call(
        kernel,
        out_shape=outs,
        grid=grid,
        scratch_shapes=list(scratch),
        compiler_params=params,
        cost_estimate=pl.CostEstimate(flops=flops, bytes_accessed=moved, transcendentals=0),
        **extra,
        **kw,
    )


def sds(shape, dtype):
    return jax.ShapeDtypeStruct(shape, dtype)


def dot(a, b):
    return lax.dot_general(a, b, (((1,), (0,)), ((), ())), preferred_element_type=f32)


def dot_nt(a, b):
    return lax.dot_general(a, b, (((1,), (1,)), ((), ())), preferred_element_type=f32)


def dot_tn(a, b):
    return lax.dot_general(a, b, (((0,), (0,)), ((), ())), preferred_element_type=f32)


def split2(v):
    high = v.astype(bf16)
    return high, (v - high.astype(f32)).astype(bf16)


def split3(v):
    high = v.astype(bf16)
    rest = v - high.astype(f32)
    mid = rest.astype(bf16)
    return high, mid, (rest - mid.astype(f32)).astype(bf16)


def iota(shape, dim):
    return lax.broadcasted_iota(jnp.int32, shape, dim)


def sigmoid(v):
    return 1.0 / (1.0 + jnp.exp(-v))


def softplus(v):
    return jnp.maximum(v, 0.0) + jnp.log1p(jnp.exp(-jnp.abs(v)))


def pair_of(v, p):
    rows = v.shape[0]
    left = jnp.broadcast_to(v[:, 2 * p : 2 * p + 1], (rows, LANES))
    right = jnp.broadcast_to(v[:, 2 * p + 1 : 2 * p + 2], (rows, LANES))
    return jnp.where(iota((rows, LANES), 1) < HDIM, left, right)


def head_mask(columns, first_head):
    return ((iota((columns, LANES), 0) >> 6) + first_head == iota((columns, LANES), 1)).astype(bf16)


def running_sum(v, reverse):
    rows, cols = iota((ROWS, ROWS), 0), iota((ROWS, ROWS), 1)
    tri = ((cols >= rows) if reverse else (cols <= rows)).astype(bf16)
    high, mid, low = split3(v)
    return dot(tri, high) + dot(tri, mid) + dot(tri, low)


def project_kernel(x_ref, gain_ref, w_ref, normed_ref, proj_ref):
    @pl.when(pl.program_id(0) == 0)
    def _():
        x = x_ref[...].astype(f32)
        scale = lax.rsqrt(jnp.mean(x * x, axis=-1, keepdims=True) + EPS)
        normed_ref[...] = (x * scale * gain_ref[...]).astype(bf16)

    proj_ref[...] = dot(normed_ref[...], w_ref[...])


def project(x, gain, weight):
    block = 512
    return call(
        project_kernel,
        (sds((ROWS, D), bf16), sds((ROWS, PROJ), f32)),
        grid=(pl.cdiv(PROJ, block),),
        in_specs=[
            pl.BlockSpec((ROWS, D), lambda k: (0, 0)),
            pl.BlockSpec((1, D), lambda k: (0, 0)),
            pl.BlockSpec((D, block), lambda k: (0, k)),
        ],
        out_specs=[
            pl.BlockSpec((ROWS, D), lambda k: (0, 0)),
            pl.BlockSpec((ROWS, block), lambda k: (0, k)),
        ],
        flops=2 * ROWS * D * PROJ,
        moved=9_500_000,
        name="project",
    )(x, gain, weight)


def conv_kernel(
    edge_ref, gain_ref, w_ref, proj_ref, dt_ref, taps_ref, bias_ref, decay_ref, dtb_ref,
    pre_ref, edge_out_ref, vbc_ref, cum_ref, step_ref, pay_ref,
    edge_n, ext, b_keep, tail_keep, states,
):
    k = pl.program_id(0)

    @pl.when(k == 0)
    def _():
        edge = edge_ref[...].astype(f32)
        scale = lax.rsqrt(jnp.mean(edge * edge, axis=-1, keepdims=True) + EPS)
        edge_n[0:8] = edge * scale * gain_ref[...]
        edge_n[8:16] = jnp.zeros((8, D), f32)
        inside = iota((ROWS, LANES), 1) < HEADS
        raw = jnp.where(inside, dt_ref[...], 0.0)
        step = jnp.where(inside, softplus(raw + dtb_ref[...]), 0.0)
        cum = running_sum(-step * jnp.exp(decay_ref[...]), False)
        step_ref[...] = step
        cum_ref[...] = cum
        tail_keep[...] = jnp.exp(cum[ROWS - 1 : ROWS] - cum)

    edge_in = dot(edge_n[...].astype(bf16), w_ref[...])[0:8]
    edge_out_ref[...] = edge_in
    ext[0:8] = edge_in
    ext[8 : 8 + ROWS] = proj_ref[...]
    total = bias_ref[...] + taps_ref[0:1] * ext[5 : 5 + ROWS]
    for tap in range(1, WIDTH):
        total = total + taps_ref[tap : tap + 1] * ext[5 + tap : 5 + tap + ROWS]
    pre_ref[...] = total
    out = total * sigmoid(total)

    @pl.when(k == 0)
    def _():
        vbc_ref[...] = out.astype(bf16)
        b_keep[...] = out[:, :NSTATE].astype(bf16)

    @pl.when(k > 0)
    def _():
        mask = head_mask(256, 4 * (k - 1))
        s_high, s_low = split2(step_ref[...])
        value = out * (dot_nt(s_high, mask) + dot_nt(s_low, mask))
        vbc_ref[...] = value.astype(bf16)
        t_high, t_low = split2(tail_keep[...])
        tailed = value * (dot_nt(t_high, mask) + dot_nt(t_low, mask))
        row = pl.multiple_of((k - 1) * 256, 256)
        states[pl.ds(row, 256), :] = dot_tn(tailed.astype(bf16), b_keep[...])

    @pl.when(k == 6)
    def _():
        total_log = cum_ref[ROWS - 1 : ROWS, :]
        piece = iota((32, LANES), 0)
        head = (piece * 48 + iota((32, LANES), 1)) >> 6
        logs = jnp.zeros((32, LANES), f32)
        for h in range(HEADS):
            logs = jnp.where(head == h, total_log[:, h : h + 1], logs)
        row16 = iota((16, LANES), 0)
        for piece in range(32):
            pay_ref[piece, 0:48, :] = states[48 * piece : 48 * piece + 48, :].astype(bf16)
            line = logs[piece : piece + 1, :]
            high = line.astype(bf16).astype(f32)
            extra = jnp.where(row16 == 0, high, jnp.where(row16 == 1, line - high, 0.0))
            pay_ref[piece, 48:64, :] = extra.astype(bf16)


def conv_states(edge, gain, weight, proj, taps, bias, decay, dtb):
    block = 256
    turn = lambda k: (k + 6) % 7
    whole = lambda k: (0, 0)
    return call(
        conv_kernel,
        (
            sds((ROWS, CONV), f32),
            sds((8, CONV), f32),
            sds((ROWS, CONV), bf16),
            sds((ROWS, LANES), f32),
            sds((ROWS, LANES), f32),
            sds((32, 64, LANES), bf16),
        ),
        scratch=[
            pltpu.VMEM((16, D), f32),
            pltpu.VMEM((ROWS + 8, block), f32),
            pltpu.VMEM((ROWS, NSTATE), bf16),
            pltpu.VMEM((ROWS, LANES), f32),
            pltpu.VMEM((INNER, NSTATE), f32),
        ],
        grid=(7,),
        in_specs=[
            pl.BlockSpec((8, D), whole),
            pl.BlockSpec((1, D), whole),
            pl.BlockSpec((D, block), lambda k: (0, 6 + turn(k))),
            pl.BlockSpec((ROWS, block), lambda k: (0, 6 + turn(k))),
            pl.BlockSpec((ROWS, LANES), lambda k: (0, 26)),
            pl.BlockSpec((WIDTH, block), lambda k: (0, turn(k))),
            pl.BlockSpec((1, block), lambda k: (0, turn(k))),
            pl.BlockSpec((1, LANES), whole),
            pl.BlockSpec((1, LANES), whole),
        ],
        out_specs=[
            pl.BlockSpec((ROWS, block), lambda k: (0, turn(k))),
            pl.BlockSpec((8, block), lambda k: (0, turn(k))),
            pl.BlockSpec((ROWS, block), lambda k: (0, turn(k))),
            pl.BlockSpec((ROWS, LANES), whole),
            pl.BlockSpec((ROWS, LANES), whole),
            pl.BlockSpec((32, 64, LANES), lambda k: (0, 0, 0)),
        ],
        flops=2 * ROWS * INNER * NSTATE + 2 * 16 * D * CONV,
        moved=9_000_000,
        name="conv_states",
    )(edge, gain, weight, proj, proj, taps, bias, decay, dtb)


def within_kernel(vbc_ref, cum_ref, y_ref, score):
    b_part = vbc_ref[:, INNER : INNER + NSTATE]
    c_part = vbc_ref[:, INNER + NSTATE :]
    keep = iota((ROWS, ROWS), 0) >= iota((ROWS, ROWS), 1)
    score[...] = jnp.where(keep, dot_nt(c_part, b_part), 0.0)
    cum = cum_ref[...]
    cum_t = jnp.transpose(cum)
    left = iota((LANES, LANES), 1) < HDIM
    for p in range(PAIRS):
        values = vbc_ref[:, p * LANES : (p + 1) * LANES]
        tops, lows = [], []
        for h in (2 * p, 2 * p + 1):
            col, row = cum[:, h : h + 1], cum_t[h : h + 1, :]
            top = jnp.exp(jnp.minimum(col[0:LANES] - row[:, 0:LANES], 0.0)) * score[0:LANES, 0:LANES]
            tops.append(dot(top.astype(bf16), values[0:LANES]))
            low = jnp.exp(jnp.minimum(col[LANES:] - row, 0.0)) * score[LANES:, :]
            lows.append(dot(low.astype(bf16), values))
        y_ref[0:LANES, p * LANES : (p + 1) * LANES] = jnp.where(left, tops[0], tops[1])
        y_ref[LANES:, p * LANES : (p + 1) * LANES] = jnp.where(left, lows[0], lows[1])


def within(vbc, cum):
    return call(
        within_kernel,
        sds((ROWS, INNER), f32),
        scratch=[pltpu.VMEM((ROWS, ROWS), f32)],
        flops=2 * HEADS * ROWS * ROWS * LANES * 4,
        moved=3_000_000,
        name="within",
    )(vbc, cum)


def scan_kernel(pay_ref, out_ref, decay_ref, logs):
    logs[...] = jnp.zeros_like(logs)
    for s in range(32):
        extra = pay_ref[s, 48:64, :].astype(f32)
        logs[s : s + 1, :] = extra[0:1] + extra[1:2]
    decay = jnp.exp(jnp.transpose(logs[...]))
    decay_ref[...] = decay
    carry = jnp.zeros((48, LANES), f32)
    for s in range(32):
        out_ref[s] = carry.astype(bf16)
        carry = decay[0:48, s : s + 1] * carry + pay_ref[s, 0:48, :].astype(f32)


def scan_states(pay):
    return call(
        scan_kernel,
        (sds((32, 48, LANES), bf16), sds((LANES, LANES), f32)),
        scratch=[pltpu.VMEM((LANES, LANES), f32)],
        moved=1_000_000,
        name="scan_states",
    )(pay)


def scan_back_kernel(grad_ref, decay_ref, out_ref):
    decay = decay_ref[...]
    carry = jnp.zeros((48, LANES), f32)
    for s in reversed(range(32)):
        out_ref[s] = carry.astype(bf16)
        carry = decay[0:48, s : s + 1] * carry + grad_ref[s].astype(f32)


def scan_back(grad, decay):
    return call(
        scan_back_kernel, sds((32, 48, LANES), bf16), moved=800_000, name="scan_back"
    )(grad, decay)


def output_kernel(
    yw_ref, c_ref, cum_ref, pre_ref, z_ref, state_ref, hid_ref, w_ref, gain_ref, skip_ref,
    hid_out, y_out, gated_ref, gate,
):
    grown = jnp.exp(cum_ref[...])
    c_part = c_ref[...]
    rows = hid_ref.shape[0]
    square = jnp.zeros((rows, 1), f32)
    for p in range(PAIRS):
        cols = slice(p * LANES, (p + 1) * LANES)
        y = yw_ref[:, cols] + dot_nt(c_part, state_ref[cols, :]) * pair_of(grown, p)
        y_out[:, cols] = y
        pre = pre_ref[:, cols]
        z = z_ref[:, cols]
        u = (y + skip_ref[:, cols] * (pre * sigmoid(pre))) * (z * sigmoid(z))
        gate[:, cols] = u
        square = square + jnp.sum(u * u, axis=-1, keepdims=True)
    scale = lax.rsqrt(square * (1.0 / INNER) + EPS)
    gated_ref[...] = (gate[...] * scale * gain_ref[...]).astype(bf16)
    hid_out[...] = hid_ref[...].astype(f32) + dot(gated_ref[...], w_ref[...])


def output_part(yw, vbc, cum, pre, proj, states, hidden, weight, gain, skip):
    rows = 128
    take = lambda k: (k, 0)
    whole = lambda k: (0, 0)
    return call(
        output_kernel,
        (sds((ROWS, D), f32), sds((ROWS, INNER), f32), sds((ROWS, INNER), bf16)),
        scratch=[pltpu.VMEM((rows, INNER), f32)],
        grid=(ROWS // rows,),
        in_specs=[
            pl.BlockSpec((rows, INNER), take),
            pl.BlockSpec((rows, LANES), lambda k: (k, 13)),
            pl.BlockSpec((rows, LANES), take),
            pl.BlockSpec((rows, INNER), take),
            pl.BlockSpec((rows, INNER), take),
            pl.BlockSpec((INNER, LANES), whole),
            pl.BlockSpec((rows, D), take),
            pl.BlockSpec((INNER, D), whole),
            pl.BlockSpec((1, INNER), whole),
            pl.BlockSpec((1, INNER), whole),
        ],
        out_specs=[
            pl.BlockSpec((rows, D), take),
            pl.BlockSpec((rows, INNER), take),
            pl.BlockSpec((rows, INNER), take),
        ],
        flops=2 * ROWS * INNER * (D + LANES),
        moved=10_000_000,
        name="output_part",
    )(yw, vbc, cum, pre, proj, states, hidden, weight, gain, skip)


def gate_back_kernel(
    grad_ref, w_ref, y_ref, z_ref, pre_ref, c_ref, cum_ref, gain_ref, skip_ref,
    low_ref, dz_ref, dy_ref, local_ref, row_ref, dgain_ref, dskip_ref,
    gate, back, high, low, heads,
):
    low_ref[...] = grad_ref[...].astype(bf16)
    back[...] = dot_nt(low_ref[...], w_ref[...])
    square = jnp.zeros((ROWS, 1), f32)
    cross = jnp.zeros((ROWS, 1), f32)
    for p in range(PAIRS):
        cols = slice(p * LANES, (p + 1) * LANES)
        pre, z = pre_ref[:, cols], z_ref[:, cols]
        u = (y_ref[:, cols] + skip_ref[:, cols] * (pre * sigmoid(pre))) * (z * sigmoid(z))
        gate[:, cols] = u
        square = square + jnp.sum(u * u, axis=-1, keepdims=True)
        cross = cross + jnp.sum(back[:, cols] * gain_ref[:, cols] * u, axis=-1, keepdims=True)
    scale = lax.rsqrt(square * (1.0 / INNER) + EPS)
    pull = scale * scale * scale * cross * (1.0 / INNER)
    grown = jnp.exp(cum_ref[...])
    for p in range(PAIRS):
        cols = slice(p * LANES, (p + 1) * LANES)
        pre, z, y = pre_ref[:, cols], z_ref[:, cols], y_ref[:, cols]
        u, grad = gate[:, cols], back[:, cols]
        x = pre * sigmoid(pre)
        dgain_ref[:, cols] = jnp.sum(grad * u * scale, axis=0, keepdims=True)
        du = grad * gain_ref[:, cols] * scale - u * pull
        sig = sigmoid(z)
        dssm = du * (z * sig)
        ssm = y + skip_ref[:, cols] * x
        dz_ref[:, cols] = (du * ssm * (sig * (1.0 + z * (1.0 - sig)))).astype(bf16)
        dy = dssm.astype(bf16)
        dy_ref[:, cols] = dy
        gate[0:1, cols] = jnp.sum(dssm * x, axis=0, keepdims=True)
        a, b = split2(dy.astype(f32) * y)
        high[:, cols] = a
        low[:, cols] = b
        heads[:, cols] = (dssm * pair_of(grown, p)).astype(bf16)
    mask = head_mask(INNER, 0)
    row_ref[...] = dot(high[...], mask) + dot(low[...], mask)
    a, b = split2(jnp.broadcast_to(gate[0:1, :], (16, INNER)))
    dskip_ref[...] = (dot(a, mask) + dot(b, mask))[0:8]
    for part in range(4):
        cols = slice(384 * part, 384 * part + 384)
        states = dot_tn(heads[:, cols], c_ref[...])
        for piece in range(8):
            local_ref[8 * part + piece] = states[48 * piece : 48 * piece + 48].astype(bf16)


def gate_back(grad, weight, y, proj, pre, vbc, cum, gain, skip):
    whole = lambda k: (0, 0)
    return call(
        gate_back_kernel,
        (
            sds((ROWS, D), bf16),
            sds((ROWS, INNER), bf16),
            sds((ROWS, INNER), bf16),
            sds((32, 48, LANES), bf16),
            sds((ROWS, LANES), f32),
            sds((1, INNER), f32),
            sds((8, LANES), f32),
        ),
        scratch=[
            pltpu.VMEM((ROWS, INNER), f32),
            pltpu.VMEM((ROWS, INNER), f32),
            pltpu.VMEM((ROWS, INNER), bf16),
            pltpu.VMEM((ROWS, INNER), bf16),
            pltpu.VMEM((ROWS, INNER), bf16),
        ],
        grid=(1,),
        in_specs=[
            pl.BlockSpec((ROWS, D), whole),
            pl.BlockSpec((INNER, D), whole),
            pl.BlockSpec((ROWS, INNER), whole),
            pl.BlockSpec((ROWS, INNER), whole),
            pl.BlockSpec((ROWS, INNER), whole),
            pl.BlockSpec((ROWS, LANES), lambda k: (0, 13)),
            pl.BlockSpec((ROWS, LANES), whole),
            pl.BlockSpec((1, INNER), whole),
            pl.BlockSpec((1, INNER), whole),
        ],
        out_specs=[
            pl.BlockSpec((ROWS, D), whole),
            pl.BlockSpec((ROWS, INNER), whole),
            pl.BlockSpec((ROWS, INNER), whole),
            pl.BlockSpec((32, 48, LANES), lambda k: (0, 0, 0)),
            pl.BlockSpec((ROWS, LANES), whole),
            pl.BlockSpec((1, INNER), whole),
            pl.BlockSpec((8, LANES), whole),
        ],
        flops=2 * ROWS * INNER * (D + LANES),
        moved=12_000_000,
        name="gate_back",
    )(grad, weight, y, proj, pre, vbc, cum, gain, skip)


def early_grads_kernel(core_ref, normed_ref, dz_ref, gated_ref, low_ref, keep_ref, send_ref):
    core = core_ref[0]
    normed_t = jnp.transpose(normed_ref[...])
    gated_t = jnp.transpose(gated_ref[...])
    for out_ref, side in ((keep_ref, core), (send_ref, 1 - core)):
        for k in range(2):
            col = pl.multiple_of((2 * k + side) * 384, LANES)
            total = dot(normed_t, dz_ref[:, pl.ds(col, 384)])
            for w in range(4):
                for rb in range(4):
                    row = 192 * w + 48 * rb
                    out_ref[4 * rb + k, w] = total[row : row + 48].astype(bf16)
        col = pl.multiple_of(side * 384, LANES)
        total = dot(gated_t, low_ref[:, pl.ds(col, 384)])
        for k in range(2):
            for w in range(4):
                for rb in range(4):
                    row = 384 * w + 192 * k + 48 * rb
                    out_ref[4 * rb + 2 + k, w] = total[row : row + 48].astype(bf16)


def early_grads(core, normed, dz, gated, low):
    shape = sds((16, 4, 48, 384), bf16)
    whole = pl.BlockSpec(memory_space=pltpu.VMEM)
    return call(
        early_grads_kernel,
        (shape, shape),
        in_specs=[pl.BlockSpec(memory_space=pltpu.SMEM)] + [whole] * 4,
        out_specs=[whole] * 2,
        flops=4 * ROWS * INNER * D,
        moved=7_000_000,
        name="early_grads",
    )(core, normed, dz, gated, low)


def within_back_kernel(vbc_ref, dy_ref, cum_ref, state_ref, dv_ref, dbc_ref, score, pile):
    b_part = vbc_ref[:, INNER : INNER + NSTATE]
    c_part = vbc_ref[:, INNER + NSTATE :]
    keep = iota((ROWS, ROWS), 0) <= iota((ROWS, ROWS), 1)
    score[...] = jnp.where(keep, dot_nt(b_part, c_part), 0.0)
    pile[...] = jnp.zeros_like(pile)
    cum = cum_ref[...]
    cum_t = jnp.transpose(cum)
    grown = jnp.exp(cum)
    left = iota((LANES, LANES), 1) < HDIM
    left_all = iota((ROWS, LANES), 1) < HDIM
    dc = jnp.zeros((ROWS, NSTATE), f32)
    for p in range(PAIRS):
        cols = slice(p * LANES, (p + 1) * LANES)
        values, dy = vbc_ref[:, cols], dy_ref[:, cols]
        tops, lows = [], []
        for side, h in enumerate((2 * p, 2 * p + 1)):
            col, row = cum[:, h : h + 1], cum_t[h : h + 1, :]
            mine = left_all if side == 0 else jnp.logical_not(left_all)
            own = jnp.where(mine, values.astype(f32), 0.0).astype(bf16)
            top = jnp.exp(jnp.minimum(row - col[0:LANES], 0.0))
            low = jnp.exp(jnp.minimum(row[:, LANES:] - col[LANES:], 0.0))
            tops.append(dot((top * score[0:LANES, :]).astype(bf16), dy))
            lows.append(dot((low * score[LANES:, LANES:]).astype(bf16), dy[LANES:]))
            pile[0:LANES, :] += top * dot_nt(own[0:LANES], dy)
            pile[LANES:, LANES:] += low * dot_nt(own[LANES:], dy[LANES:])
        dv_ref[0:LANES, cols] = jnp.where(left, tops[0], tops[1])
        dv_ref[LANES:, cols] = jnp.where(left, lows[0], lows[1])
        lifted = (dy.astype(f32) * pair_of(grown, p)).astype(bf16)
        dc = dc + dot(lifted, state_ref[cols, :])
    dscore = jnp.where(keep, pile[...], 0.0).astype(bf16)
    dbc_ref[:, 0:NSTATE] = dot(dscore, c_part)
    dbc_ref[:, NSTATE:] = dc + dot_tn(dscore, b_part)


def within_back(vbc, dy, cum, states):
    return call(
        within_back_kernel,
        (sds((ROWS, INNER), f32), sds((ROWS, 2 * NSTATE), f32)),
        scratch=[pltpu.VMEM((ROWS, ROWS), f32), pltpu.VMEM((ROWS, ROWS), f32)],
        flops=2 * HEADS * ROWS * ROWS * LANES * 6,
        moved=4_000_000,
        name="within_back",
    )(vbc, dy, cum, states)


def conv_back_kernel(
    later_ref, state_ref, dv_ref, dy_ref, vbc_ref, pre_ref, proj_ref, edge_ref, taps_ref, skip_ref,
    b_ref, cum_ref, step_ref, dt_ref, dbc_ref, row_ref, decay_ref, dtb_ref,
    pg_ref, edge_grad_ref, param_ref, ddt_ref, vec_ref,
    ext_in, ext_out, tail_keep, acc_b, acc_v, acc_x, acc_t, acc_s,
):
    k = pl.program_id(0)

    @pl.when(k == 0)
    def _():
        cum = cum_ref[...]
        tail_keep[...] = jnp.exp(cum[ROWS - 1 : ROWS] - cum)
        acc_b[...] = jnp.zeros_like(acc_b)
        acc_v[...] = jnp.zeros_like(acc_v)
        acc_x[...] = jnp.zeros_like(acc_x)
        acc_t[...] = jnp.zeros_like(acc_t)
        acc_s[...] = jnp.zeros_like(acc_s)
        ext_out[0:8] = jnp.zeros((8, 256), f32)
        ext_out[ROWS + 8 :] = jnp.zeros((8, 256), f32)

    pre = pre_ref[...]
    sig = sigmoid(pre)

    @pl.when(k < 6)
    def _():
        mask = head_mask(256, 4 * k)
        high, low = split2(step_ref[...])
        step = dot_nt(high, mask) + dot_nt(low, mask)
        high, low = split2(tail_keep[...])
        tail = dot_nt(high, mask) + dot_nt(low, mask)
        later = later_ref[...]
        value = vbc_ref[...].astype(f32)
        acc_b[...] += dot((value * tail).astype(bf16), later)
        from_state = tail * dot_nt(b_ref[...], later)
        dv = dv_ref[...] + from_state
        x = pre * sig
        high, low = split2(value * dv)
        acc_v[...] += dot(high, mask) + dot(low, mask)
        high, low = split2(x * dv)
        acc_x[...] += dot(high, mask) + dot(low, mask)
        sums = jnp.broadcast_to(jnp.sum(value * from_state, axis=0, keepdims=True), (16, 256))
        high, low = split2(sums)
        acc_t[...] += (dot(high, mask) + dot(low, mask))[0:8]
        high, low = split2(later.astype(f32) * state_ref[...].astype(f32))
        ones = jnp.ones((16, NSTATE), bf16)
        high, low = split2(dot_nt(ones, high) + dot_nt(ones, low))
        acc_s[...] += (dot(high, mask) + dot(low, mask))[0:8]
        ext_out[8 : 8 + ROWS] = step * dv + skip_ref[...] * dy_ref[...].astype(f32)

    @pl.when(k == 6)
    def _():
        ext_out[8 : 8 + ROWS, 0:NSTATE] = dbc_ref[:, 0:NSTATE] + acc_b[...]
        ext_out[8 : 8 + ROWS, NSTATE:] = dbc_ref[:, NSTATE:]
        inside = iota((ROWS, LANES), 1) < HEADS
        raw = jnp.where(inside, dt_ref[...], 0.0) + dtb_ref[...]
        rate = jnp.exp(decay_ref[...])
        log_decay = -step_ref[...] * rate
        whole = acc_t[0:1] + jnp.exp(cum_ref[ROWS - 1 : ROWS]) * acc_s[0:1]
        dlog = running_sum(row_ref[...] - acc_v[...], True) + whole
        dstep = acc_x[...] - dlog * rate
        ddt = jnp.where(inside, dstep * sigmoid(raw), 0.0)
        ddt_ref[...] = ddt.astype(bf16)
        vec_ref[0:1] = jnp.sum(jnp.where(inside, dlog * log_decay, 0.0), axis=0, keepdims=True)
        vec_ref[1:2] = jnp.sum(ddt, axis=0, keepdims=True)
        vec_ref[2:8] = jnp.zeros((6, LANES), f32)

    ds = ext_out[8 : 8 + ROWS] * (sig * (1.0 + pre * (1.0 - sig)))
    ext_out[8 : 8 + ROWS] = ds
    ext_in[0:8] = edge_ref[...]
    ext_in[8 : 8 + ROWS] = proj_ref[...]
    grad = taps_ref[3:4] * ds
    edge_grad = taps_ref[3:4] * ext_out[0:8]
    param_ref[3:4] = jnp.sum(ds * ext_in[8 : 8 + ROWS], axis=0, keepdims=True)
    for tap in range(WIDTH - 1):
        ahead = WIDTH - 1 - tap
        weight = taps_ref[tap : tap + 1]
        grad = grad + weight * ext_out[8 + ahead : 8 + ahead + ROWS]
        edge_grad = edge_grad + weight * ext_out[ahead : ahead + 8]
        param_ref[tap : tap + 1] = jnp.sum(ds * ext_in[5 + tap : 5 + tap + ROWS], axis=0, keepdims=True)
    param_ref[4:5] = jnp.sum(ds, axis=0, keepdims=True)
    param_ref[5:8] = jnp.zeros((3, 256), f32)
    pg_ref[...] = grad
    edge_grad_ref[...] = edge_grad


def conv_back(later, states, dv, dy, vbc, pre, proj, edge, taps, skip, cum, step, dbc, row, decay, dtb):
    block = 256
    upto = lambda k: jnp.minimum(k, 5)
    whole = lambda k: (0, 0)
    return call(
        conv_back_kernel,
        (
            sds((ROWS, CONV), f32),
            sds((8, CONV), f32),
            sds((8, CONV), f32),
            sds((ROWS, LANES), bf16),
            sds((8, LANES), f32),
        ),
        scratch=[
            pltpu.VMEM((ROWS + 8, block), f32),
            pltpu.VMEM((ROWS + 16, block), f32),
            pltpu.VMEM((ROWS, LANES), f32),
            pltpu.VMEM((ROWS, NSTATE), f32),
            pltpu.VMEM((ROWS, LANES), f32),
            pltpu.VMEM((ROWS, LANES), f32),
            pltpu.VMEM((8, LANES), f32),
            pltpu.VMEM((8, LANES), f32),
        ],
        grid=(7,),
        in_specs=[
            pl.BlockSpec((block, NSTATE), lambda k: (upto(k), 0)),
            pl.BlockSpec((block, NSTATE), lambda k: (upto(k), 0)),
            pl.BlockSpec((ROWS, block), lambda k: (0, upto(k))),
            pl.BlockSpec((ROWS, block), lambda k: (0, upto(k))),
            pl.BlockSpec((ROWS, block), lambda k: (0, k)),
            pl.BlockSpec((ROWS, block), lambda k: (0, k)),
            pl.BlockSpec((ROWS, block), lambda k: (0, 6 + k)),
            pl.BlockSpec((8, block), lambda k: (0, k)),
            pl.BlockSpec((WIDTH, block), lambda k: (0, k)),
            pl.BlockSpec((1, block), lambda k: (0, upto(k))),
            pl.BlockSpec((ROWS, NSTATE), lambda k: (0, 12)),
            pl.BlockSpec((ROWS, LANES), whole),
            pl.BlockSpec((ROWS, LANES), whole),
            pl.BlockSpec((ROWS, LANES), lambda k: (0, 26)),
            pl.BlockSpec((ROWS, 2 * NSTATE), whole),
            pl.BlockSpec((ROWS, LANES), whole),
            pl.BlockSpec((1, LANES), whole),
            pl.BlockSpec((1, LANES), whole),
        ],
        out_specs=[
            pl.BlockSpec((ROWS, block), lambda k: (0, k)),
            pl.BlockSpec((8, block), lambda k: (0, k)),
            pl.BlockSpec((8, block), lambda k: (0, k)),
            pl.BlockSpec((ROWS, LANES), whole),
            pl.BlockSpec((8, LANES), whole),
        ],
        flops=6 * ROWS * INNER * NSTATE,
        moved=12_000_000,
        name="conv_back",
    )(
        later, states, dv, dy, vbc, pre, proj, edge, taps, skip,
        vbc, cum, step, proj, dbc, row, decay, dtb,
    )


def norm_back_kernel(
    pg_ref, next_ref, dz_ref, ddt_ref, w_ref, x_ref, gain_ref, grad_ref,
    low_ref, out_ref, dgain_ref,
):
    low_ref[0 : ROWS - 16] = pg_ref[0 : ROWS - 16].astype(bf16)
    last = pg_ref[ROWS - 16 :]
    low_ref[ROWS - 16 :] = jnp.concatenate([last[0:8], last[8:16] + next_ref[...]]).astype(bf16)
    back = dot_nt(dz_ref[...], w_ref[:, 0:INNER])
    back = back + dot_nt(low_ref[...], w_ref[:, INNER : INNER + CONV])
    back = back + dot_nt(ddt_ref[:, 0:HEADS], w_ref[:, INNER + CONV : PROJ])
    x = x_ref[...].astype(f32)
    scale = lax.rsqrt(jnp.mean(x * x, axis=-1, keepdims=True) + EPS)
    dgain_ref[...] = jnp.sum(back * x * scale, axis=0, keepdims=True)
    scaled = back * gain_ref[...]
    pull = scale * scale * scale * jnp.mean(scaled * x, axis=-1, keepdims=True)
    out_ref[...] = grad_ref[...].astype(f32) + scaled * scale - x * pull


def norm_back(pg, following, dz, ddt, weight, x, gain, grad):
    return call(
        norm_back_kernel,
        (sds((ROWS, CONV), bf16), sds((ROWS, D), f32), sds((1, D), f32)),
        flops=2 * ROWS * D * PROJ,
        moved=11_000_000,
        name="norm_back",
    )(pg, following, dz, ddt, weight, x, gain, grad)


def late_grads_kernel(
    core_ref, normed_ref, low_ref, ddt_ref, dgain_in_ref, dgain_out_ref, param_ref, vec_ref, dskip_ref,
    keep_ref, send_ref, small,
):
    core = core_ref[0]
    small[...] = jnp.zeros_like(small)
    line = 0
    for ref, first, count in ((dgain_in_ref, 0, 6), (dgain_out_ref, 0, 12)):
        for i in range(count):
            small[line : line + 1, :] = ref[first : first + 1, LANES * i : LANES * i + LANES]
            line += 1
    for tap in range(WIDTH + 1):
        for i in range(CONV // LANES):
            small[line : line + 1, :] = param_ref[tap : tap + 1, LANES * i : LANES * i + LANES]
            line += 1
    vec = vec_ref[...]
    lane = iota((8, LANES), 1)
    decay = jnp.where(lane < HEADS, jnp.broadcast_to(vec[0:1], (8, LANES)), 0.0)
    dtb = jnp.where(lane < HEADS, jnp.broadcast_to(vec[1:2], (8, LANES)), 0.0)
    skip = jnp.where(lane < HEADS, dskip_ref[...], 0.0)
    joined = decay + pltpu.roll(dtb, HEADS, 1) + pltpu.roll(skip, 2 * HEADS, 1)
    small[line : line + 1, :] = joined[0:1]

    normed_t = jnp.transpose(normed_ref[...])

    def place(out_ref, k, lanes, total):
        for w in range(4):
            for rb in range(4):
                row = 192 * w + 48 * rb
                out_ref[4 * rb + k, w, :, lanes] = total[row : row + 48].astype(bf16)

    for out_ref, side in ((keep_ref, core), (send_ref, 1 - core)):
        for k in range(3):
            col = pl.multiple_of((2 * k + side) * 256, LANES)
            place(out_ref, k, slice(0, 256), dot(normed_t, low_ref[:, pl.ds(col, 256)]))

        @pl.when(side == 0)
        def _(out_ref=out_ref):
            place(out_ref, 3, slice(0, 256), dot(normed_t, low_ref[:, 1536:1792]))

        @pl.when(side == 1)
        def _(out_ref=out_ref):
            place(out_ref, 3, slice(0, 128), dot(normed_t, ddt_ref[...]))
            for w in range(4):
                for rb in range(4):
                    if rb < 2:
                        block = small[48 * rb : 48 * rb + 48, :]
                    else:
                        block = jnp.zeros((48, LANES), f32)
                    out_ref[4 * rb + 3, w, :, 128:256] = block.astype(bf16)


def late_grads(core, normed, low, ddt, dgain_in, dgain_out, param, vec, dskip):
    shape = sds((16, 4, 48, 256), bf16)
    whole = pl.BlockSpec(memory_space=pltpu.VMEM)
    return call(
        late_grads_kernel,
        (shape, shape),
        scratch=[pltpu.VMEM((96, LANES), f32)],
        in_specs=[pl.BlockSpec(memory_space=pltpu.SMEM)] + [whole] * 8,
        out_specs=[whole] * 2,
        flops=2 * ROWS * D * CONV,
        moved=5_000_000,
        name="late_grads",
    )(core, normed, low, ddt, dgain_in, dgain_out, param, vec, dskip)


def adam_step(weight, moment, second, gradient, learn_rate, weight_decay):
    new_moment = 0.9 * moment + 0.1 * gradient
    new_second = 0.95 * second + 0.05 * gradient * gradient
    corrected = new_moment / (1.0 - 0.9**STEP) / (jnp.sqrt(new_second / (1.0 - 0.95**STEP)) + 1e-08)
    return (new_moment, new_second, weight - learn_rate * (corrected + weight_decay * weight))


def adam_in_kernel(zo_ref, cs_ref, w_ref, m_ref, v_ref, *refs):
    m_out, v_out, w_out = refs[-3:]

    def update(first, width, grad):
        cols = slice(first, first + width)
        new_m, new_v, new_w = adam_step(
            w_ref[0, :, cols], m_ref[0, :, cols], v_ref[0, :, cols], grad.astype(f32), 0.03, 0.1
        )
        m_out[0, :, cols] = new_m
        v_out[0, :, cols] = new_v
        w_out[0, :, cols] = new_w

    for cb in range(4):
        update(384 * cb, 384, zo_ref[0, cb])
    for cb in range(7):
        update(INNER + 256 * cb, 256, cs_ref[0, cb])
    update(INNER + CONV, HEADS, cs_ref[0, 7][:, 0:HEADS])


def adam_in(zo, cs, w, m, v, layer, before):
    state = pl.BlockSpec((1, 48, PROJ), lambda r: (layer, r, 0))
    shape = sds((2, 192, PROJ), f32)
    aliases = {} if before is None else {5: 0, 6: 1, 7: 2}
    held = () if before is None else tuple(before)
    return call(
        adam_in_kernel,
        (shape, shape, shape),
        grid=(4,),
        in_specs=[
            pl.BlockSpec((1, 8, 48, 384), lambda r: (r, 0, 0, 0)),
            pl.BlockSpec((1, 8, 48, 256), lambda r: (r, 0, 0, 0)),
            state,
            state,
            state,
        ]
        + [pl.BlockSpec(memory_space=pl.ANY)] * len(held),
        out_specs=[state] * 3,
        input_output_aliases=aliases,
        moved=17_000_000,
        name="adam_in",
    )(zo, cs, w, m, v, *held)


def adam_out_kernel(zo_ref, w_ref, m_ref, v_ref, *refs):
    m_out, v_out, w_out = refs[-3:]
    for half in range(2):
        for cb in range(2):
            cols = slice(384 * cb, 384 * cb + 384)
            new_m, new_v, new_w = adam_step(
                w_ref[0, half, :, cols], m_ref[0, half, :, cols], v_ref[0, half, :, cols],
                zo_ref[0, 4 + 2 * half + cb].astype(f32), 0.02, 0.1,
            )
            m_out[0, half, :, cols] = new_m
            v_out[0, half, :, cols] = new_v
            w_out[0, half, :, cols] = new_w


def adam_out(zo, w, m, v, layer, before):
    state = pl.BlockSpec((1, 2, 48, D), lambda r: (layer, 0, r, 0))
    shape = sds((2, 2, 192, D), f32)
    aliases = {} if before is None else {4: 0, 5: 1, 6: 2}
    held = () if before is None else tuple(before)
    return call(
        adam_out_kernel,
        (shape, shape, shape),
        grid=(4,),
        in_specs=[
            pl.BlockSpec((1, 8, 48, 384), lambda r: (r, 0, 0, 0)),
            state,
            state,
            state,
        ]
        + [pl.BlockSpec(memory_space=pl.ANY)] * len(held),
        out_specs=[state] * 3,
        input_output_aliases=aliases,
        moved=8_000_000,
        name="adam_out",
    )(zo, w, m, v, *held)


def next_in_sequence(rows, step):
    route = [(i, i + step) for i in range(32) if 0 <= i + step < 32]
    return lax.ppermute(rows, PLANE, route)


def exchange(blocks):
    return lax.all_to_all(blocks, PLANE, 0, 0, tiled=True)


def reduce_pieces(keep, send):
    received = lax.ppermute(send, "core", [(0, 1), (1, 0)])
    paired = (keep.astype(f32) + received.astype(f32)).astype(bf16)
    width = keep.shape[-1]
    parts = lax.all_to_all(paired.reshape(64, 48, width), ("x", "z", "wt"), 0, 0, tiled=True)
    total = jnp.sum(parts.astype(f32), axis=0).astype(bf16)
    spread = exchange(jnp.broadcast_to(total[None], (32, 48, width)))
    return spread.reshape(4, 8, 48, width)


def shards(
    tokens, in_w, in_m, in_v, out_w, out_m, out_v, small_params, small_m, small_v, cotangent
):
    core = lax.axis_index("core").astype(jnp.int32).reshape(1)
    tokens = tokens[0]
    cotangent = cotangent[0]
    in_full, out_full = [], []
    for layer in range(2):
        in_full.append(lax.all_gather(in_w[layer].astype(bf16), "wt", axis=0, tiled=True))
        out_full.append(lax.all_gather(out_w[layer].astype(bf16), "wt", axis=0, tiled=True))
    small_full = lax.all_gather(small_params.astype(bf16), "wt", axis=1, tiled=True).astype(f32)

    def heads_row(first):
        return jnp.pad(small_full[:, first : first + HEADS], ((0, 0), (0, LANES - HEADS)))

    gain_in = small_full[:, :D]
    gain_out = small_full[:, D : D + INNER]
    taps = small_full[:, 2304:9472].reshape(2, WIDTH, CONV)
    bias = small_full[:, 9472:11264]
    decay = heads_row(11264)
    dtb = heads_row(11264 + HEADS)
    skip = jnp.repeat(small_full[:, 11264 + 2 * HEADS : VEC], HDIM, axis=1)

    hidden = tokens
    saved = []
    for layer in range(2):
        row = slice(layer, layer + 1)
        edge = next_in_sequence(hidden[ROWS - 8 :], 1)
        normed, proj = project(hidden, gain_in[row], in_full[layer])
        pre, edge_in, vbc, cum, step, pay = conv_states(
            edge, gain_in[row], in_full[layer], proj, taps[layer], bias[row], decay[row], dtb[row]
        )
        slices = exchange(pay)
        yw = within(vbc, cum)
        scanned, chain = scan_states(slices)
        states = exchange(scanned).reshape(INNER, NSTATE)
        after, y, gated = output_part(
            yw, vbc, cum, pre, proj, states, hidden, out_full[layer], gain_out[row], skip[row]
        )
        saved.append((hidden, normed, proj, pre, edge_in, vbc, cum, step, chain, states, y, gated))
        hidden = after

    grad = cotangent
    reduced = [None, None]
    for layer in (1, 0):
        row = slice(layer, layer + 1)
        start, normed, proj, pre, edge_in, vbc, cum, step, chain, states, y, gated = saved[layer]
        low, dz, dy, local, rows_sum, dgain_out, dskip = gate_back(
            grad, out_full[layer], y, proj, pre, vbc, cum, gain_out[row], skip[row]
        )
        slices = exchange(local)
        dv, dbc = within_back(vbc, dy, cum, states)
        early = early_grads(core, normed, dz, gated, low)
        later = exchange(scan_back(slices, chain)).reshape(INNER, NSTATE)
        pg, edge_grad, param, ddt, vec = conv_back(
            later, states, dv, dy, vbc, pre, proj, edge_in, taps[layer], skip[row],
            cum, step, dbc, rows_sum, decay[row], dtb[row],
        )
        following = next_in_sequence(edge_grad, -1)
        pg_low, grad, dgain_in = norm_back(
            pg, following, dz, ddt, in_full[layer], start, gain_in[row], grad
        )
        late = late_grads(core, normed, pg_low, ddt, dgain_in, dgain_out, param, vec, dskip)
        reduced[layer] = (reduce_pieces(*early), reduce_pieces(*late))

    split = lambda a: a.reshape(2, 2, 192, D)
    new_in, new_out = None, None
    for layer in (1, 0):
        zo, cs = reduced[layer]
        new_in = adam_in(zo, cs, in_w, in_m, in_v, layer, new_in)
        new_out = adam_out(zo, split(out_w), split(out_m), split(out_v), layer, new_out)
    small_total = jnp.stack([cs[0:2, 7, :, 128:256].reshape(96 * LANES)[:VEC] for _, cs in reduced])
    width = VEC // 4
    small_total = lax.dynamic_slice_in_dim(
        small_total.astype(f32), lax.axis_index("wt") * width, width, 1
    )
    new_small = adam_step(small_params, small_m, small_v, small_total, 0.2, 0.0)
    return (
        hidden[None],
        grad[None],
        *new_in,
        *(a.reshape(2, 384, D) for a in new_out),
        *new_small,
    )


def solution(mesh):
    fine = Mesh(mesh.devices.reshape(4, 4, 2, 4), ("x", "z", "core", "wt"))
    rows = P("wt", PLANE, None)
    held = P(None, "wt", None)
    flat = P(None, "wt")
    return jax.shard_map(
        shards,
        mesh=fine,
        in_specs=(rows, held, held, held, held, held, held, flat, flat, flat, rows),
        out_specs=(rows, rows, held, held, held, held, held, held, flat, flat, flat),
        check_vma=False,
    )
```

time: 1410 us -> 641 us (0.45)
  other arithmetic: 485 us -> 28.5 us
  blocking collectives: 381 us -> 58.9 us
  matrix products: 152 us -> 0 us
  Pallas kernels: 0 us -> 138 us
  starting transfers between devices: 16.2 us -> 86.5 us
  local copies, waits for them, and re-layouts: 152 us -> 83.7 us
  waiting for transfers between devices: 186 us -> 218 us
    unnamed x4 -> x0, blocking collectives: 371 us -> none
    select_n x126 -> x0, other arithmetic: 228 us -> none  [the longest x62 116 us: step(): jnp.where(position < mine, new, old)]
    dot_general x46 -> x0, matrix products: 152 us -> none  [the longest x6 50 us: one_block(): jnp.einsum('hij,jhp->ihp', weight_mat, heads_block, precision=highest)]
    pallas_call x0 -> x28, Pallas kernels: none -> 138 us  [the longest x2 22.8 us: conv_back(): call(conv_back_kernel, (sds((ROWS, CONV), f32), sds((8, CONV), f32), sds(...]
    all_to_all x0 -> x13, waiting for transfers between devices: none -> 135 us  [the longest x9 70.7 us: exchange(): return lax.all_to_all(blocks, PLANE, 0, 0, tiled=True)]
    all_gather x10 -> x4, waiting for transfers between devices: 185 us -> 68.8 us  [the longest x2 68.8 us: shards(): lax.all_gather(in_w[layer].astype(bf16), 'wt', axis=0, tiled=True)]
    add x67 -> x0, other arithmetic: 77.5 us -> none  [the longest x60 71.8 us: chain_step(): later[0][:, None, None] * earlier[1] + later[1]]
    all_to_all x0 -> x13, starting transfers between devices: none -> 72.4 us  [the longest x9 49.1 us: exchange(): return lax.all_to_all(blocks, PLANE, 0, 0, tiled=True)]
  transfers between devices with their start and end apart: 15 -> 25, of which waited for: 6 -> 16; matrix products, arithmetic and copies ran while one was open for 34% -> 6% of each run, Pallas kernels for 0% -> 15%
where the time goes in v1:
time: 641 us; the launch traced here: 629 us
  waiting for transfers between devices  218 us (34%)
  Pallas kernels  138 us (22%)
  starting transfers between devices  86.5 us (13%)
  local copies, waits for them, and re-layouts  83.7 us (13%)
  blocking collectives  58.9 us (9%)
  other arithmetic  28.5 us (4%)
  between operations  15.2 us (2%)
    all_to_all x9, waiting for transfers between devices, exchange(): return lax.all_to_all(blocks, PLANE, 0, 0, tiled=True)  70.7 us
    all_gather x2, waiting for transfers between devices, shards(): lax.all_gather(in_w[layer].astype(bf16), 'wt', axis=0, tiled=True)  68.8 us
    unnamed x244, local copies, waits for them, and re-layouts  67.8 us
    all_to_all x4, waiting for transfers between devices, reduce_pieces(): lax.all_to_all(paired.reshape(64, 48, width), ('x', 'z', 'wt'), 0, 0, til...  64.4 us
    all_to_all x3, blocking collectives, exchange(): return lax.all_to_all(blocks, PLANE, 0, 0, tiled=True)  49.4 us
    all_to_all x9, starting transfers between devices, exchange(): return lax.all_to_all(blocks, PLANE, 0, 0, tiled=True)  49.1 us
    all_to_all x4, starting transfers between devices, reduce_pieces(): lax.all_to_all(paired.reshape(64, 48, width), ('x', 'z', 'wt'), 0, 0, til...  23.3 us
    pallas_call x2, Pallas kernels, conv_back(): call(conv_back_kernel, (sds((ROWS, CONV), f32), sds((8, CONV), f32), sds(...  22.8 us
  transfers between devices with their start and end apart: 25, of which 16 were waited for; matrix products, arithmetic and copies ran while one was open for 6% of the time, Pallas kernels for 15%

profile of v1, /device:TPU:1, one launch (start us, length us, event | category | flops | bytes accessed | tf_op | source)
XLA Modules:
  0.0 628.8 jit_solution(3535448238659215992)
XLA Ops:
  14.7 4.9 collective-permute-start
  19.7 9.5 %all-gather.4 = bf16[4,2834,2]{1,2,0:T(2,128)(2,1)S(1)} all-gather(bf16[1,2834,2]{1,2,0:T(2,128)(2,1)S(1)} %convert_bitcast_fusion), channel_id=1, replica_groups=mesh['x'=4,'z'=4,'core'=2,'wt'=4] {'wt'}, dimensions={0}, use_global_device_ids=true | all-gather | bytes 56680 | tf_op jit(solution)/shard_map/all_gather | solution.py:905
  30.9 41.8 %all-gather.10.cloned.1.call-done = bf16[1,768,3352]{2,1,0:T(8,128)(2,1)} async-done(((bf16[1,192,3352]{2,1,0:T(8,128)(2,1)}), bf16[1,768,3352]{2,1,0:T(8,128)(2,1)}) %all-gather.10.cloned.1.call-update) | async-done | bytes 5148688 | tf_op jit(solution)/shard_map/all_gather | solution.py:903
  72.7 6.4 %project.2 = (bf16[256,768]{1,0:T(8,128)(2,1)S(1)}, f32[256,3352]{1,0:T(8,128)S(1)}) custom-call(bf16[256,768]{1,0:T(8,128)(2,1)S(1)} %bitcast.50, f32[1,768]{1,0:T(1,128)S(1)} %get-tuple-element.187.gain_ref, bf16[768,3352]{1,0:T(8,128)(2,1)} %bitcast.62), custom_call_target="tpu_custom_call" | custom-call | flops 1318060032 | bytes 9500000 | tf_op jit(solution)/shard_map/project/pallas_call | solution.py:120
  81.7 8.5 %conv_states.2 = (f32[256,1792]{1,0:T(8,128)S(1)}, f32[8,1792]{1,0:T(8,128)S(1)}, bf16[256,1792]{1,0:T(8,128)(2,1)S(1)}, f32[256,128]{1,0:T(8,128)S(1)}, f32[256...) custom-call(bf16[8,768]{1,0:T(8,128)(2,1)S(1)} %collective-permute-done.edge_ref, ...), custom_call_target="tpu_custom_call" | custom-call | flops 144703488 | bytes 9000000 | tf_op jit(solution)/shard_map/conv_states/pallas_call | solution.py:207
  93.5 7.8 %all-to-all-start = ((bf16[32,64,128]{2,1,0:T(8,128)(2,1)}), bf16[32,64,128]{2,1,0:T(8,128)(2,1)}, u32[]{:S(2)}, u32[]{:S(2)}) async-start(bf16[32,64,128]{2,1,0:T(8,128)(2,1)} %copy-done.54), calls=%async_computation | async-start | bytes 1048576 | tf_op jit(solution)/shard_map/all_to_all | solution.py:882
  103.4 9.5 %all-to-all-done.pay_ref = bf16[32,64,128]{2,1,0:T(8,128)(2,1)} async-done(((bf16[32,64,128]{2,1,0:T(8,128)(2,1)}), bf16[32,64,128]{2,1,0:T(8,128)(2,1)}, u32[]{:S(2)}, u32[]{:S(2)}) %all-to-all-start) | async-done | bytes 524320 | tf_op jit(solution)/shard_map/all_to_all | solution.py:882
  115.2 4.4 all-to-all-start.1
  123.5 6.2 all-to-all-done.1
  130.7 5.8 output_part.2
  141.4 27.0 %all-gather.14.cloned.1.call-done = bf16[1,768,3352]{2,1,0:T(8,128)(2,1)} async-done(((bf16[1,192,3352]{2,1,0:T(8,128)(2,1)}), bf16[1,768,3352]{2,1,0:T(8,128)(2,1)}) %all-gather.14.cloned.1.call-update) | async-done | bytes 5148688 | tf_op jit(solution)/shard_map/all_gather | solution.py:903
  169.5 6.4 %project.3 = (bf16[256,768]{1,0:T(8,128)(2,1)S(1)}, f32[256,3352]{1,0:T(8,128)S(1)}) custom-call(f32[256,768]{1,0:T(8,128)S(1)} %copy-done.14, f32[1,768]{1,0:T(1,128)S(1)} %get-tuple-element.186.gain_ref, bf16[768,3352]{1,0:T(8,128)(2,1)} %bitcast.59), custom_call_target="tpu_custom_call" | custom-call | flops 1318060032 | bytes 9500000 | tf_op jit(solution)/shard_map/project/pallas_call | solution.py:120
  179.9 8.4 %conv_states.3 = (f32[256,1792]{1,0:T(8,128)S(1)}, f32[8,1792]{1,0:T(8,128)S(1)}, bf16[256,1792]{1,0:T(8,128)(2,1)S(1)}, f32[256,128]{1,0:T(8,128)S(1)}, f32[256...) custom-call(f32[8,768]{1,0:T(8,128)S(1)} %copy-done.88, f32[1,768]{1,0:T(1,128)S(1)} %get-tuple-element.186.gain_ref, ...), custom_call_target="tpu_custom_call" | custom-call | flops 144703488 | bytes 9000000 | tf_op jit(solution)/shard_map/conv_states/pallas_call | solution.py:207
  190.5 19.2 %all_to_all.80.pay_ref = bf16[32,64,128]{2,1,0:T(8,128)(2,1)S(1)} all-to-all(bf16[32,64,128]{2,1,0:T(8,128)(2,1)S(1)} %get-tuple-element.102), channel_id=1, replica_groups=mesh['x'=4,'z'=4,'core'=2,'wt'=4] {'x','z','core'}, dimensions={0} | all-to-all | bytes 1048576 | tf_op jit(solution)/shard_map/all_to_all | solution.py:882
  211.5 4.6 all-to-all-start.3
  221.3 5.0 all-to-all-done.3
  230.6 6.5 %output_part.3 = (f32[256,768]{1,0:T(8,128)}, f32[256,1536]{1,0:T(8,128)S(1)}, bf16[256,1536]{1,0:T(8,128)(2,1)S(1)}) custom-call(f32[256,1536]{1,0:T(8,128)S(1)} %copy-done.33, bf16[256,1792]{1,0:T(8,128)(2,1)S(1)} %copy-done.7, f32[256,128]{1,0:T(8,128)S(1)} %get-tuple-element.100.cum_ref, f32[256,1792]{1,0:T(8,128)} %copy-done.4, f32[256,3352]{1,0:T(8,128)} %copy-done.1, ...), custom_call_target="tpu_custom_call" | custom-call | flops 704643072 | bytes 10000000 | tf_op jit(solution)/shard_map/output_part/pallas_call | solution.py:345
  238.0 7.4 %gate_back.2 = (bf16[256,768]{1,0:T(8,128)(2,1)S(1)}, bf16[256,1536]{1,0:T(8,128)(2,1)S(1)}, bf16[256,1536]{1,0:T(8,128)(2,1)S(1)}, bf16[32,48,128]{2,1,0:T(8,12...) custom-call(bf16[256,768]{1,0:T(8,128)(2,1)S(1)} %bitcast.57, ...), custom_call_target="tpu_custom_call" | custom-call | flops 704643072 | bytes 12000000 | tf_op jit(solution)/shard_map/gate_back/pallas_call | solution.py:423
  249.0 13.6 %all_to_all.81.grad_ref = bf16[32,48,128]{2,1,0:T(8,128)(2,1)S(1)} all-to-all(bf16[32,48,128]{2,1,0:T(8,128)(2,1)S(1)} %get-tuple-element.106), channel_id=1, replica_groups=mesh['x'=4,'z'=4,'core'=2,'wt'=4] {'x','z','core'}, dimensions={0} | all-to-all | bytes 786432 | tf_op jit(solution)/shard_map/all_to_all | solution.py:882
  263.7 4.8 all-to-all-start.5
  288.0 11.3 %conv_back.2 = (f32[256,1792]{1,0:T(8,128)}, f32[8,1792]{1,0:T(8,128)}, f32[8,1792]{1,0:T(8,128)S(1)}, bf16[256,128]{1,0:T(8,128)(2,1)S(1)}, f32[8,128]{1,0:T(8,128)S(1)}) custom-call(bf16[1536,128]{1,0:T(8,128)(2,1)} %bitcast.15.later_ref, bf16[1536,128]{1,0:T(8,128)(2,1)} %bitcast.10.state_ref, f32[256,1536]{1,0:T(8,128)S(1)} %copy-done.41, ...), custom_call_target="tpu_custom_call" | custom-call | flops 301989888 | bytes 12000000 | tf_op jit(solution)/shard_map/conv_back/pallas_call | solution.py:638
  313.2 4.4 norm_back.2
  326.8 7.5 %gate_back.3 = (bf16[256,768]{1,0:T(8,128)(2,1)S(1)}, bf16[256,1536]{1,0:T(8,128)(2,1)S(1)}, bf16[256,1536]{1,0:T(8,128)(2,1)S(1)}, bf16[32,48,128]{2,1,0:T(8,12...) custom-call(f32[256,768]{1,0:T(8,128)S(1)} %get-tuple-element.118.grad_ref, ...), custom_call_target="tpu_custom_call" | custom-call | flops 704643072 | bytes 12000000 | tf_op jit(solution)/shard_map/gate_back/pallas_call | solution.py:423
  336.6 16.6 %all_to_all.82.grad_ref = bf16[32,48,128]{2,1,0:T(8,128)(2,1)S(1)} all-to-all(bf16[32,48,128]{2,1,0:T(8,128)(2,1)S(1)} %get-tuple-element.120), channel_id=1, replica_groups=mesh['x'=4,'z'=4,'core'=2,'wt'=4] {'x','z','core'}, dimensions={0} | all-to-all | bytes 786432 | tf_op jit(solution)/shard_map/all_to_all | solution.py:882
  354.2 4.4 all-to-all-start.7
  362.2 6.6 %all-to-all-done.7 = bf16[32,48,128]{2,1,0:T(8,128)(2,1)} async-done(((bf16[32,48,128]{2,1,0:T(8,128)(2,1)}), bf16[32,48,128]{2,1,0:T(8,128)(2,1)}, u32[]{:S(2)}, u32[]{:S(2)}) %all-to-all-start.7) | async-done | bytes 393248 | tf_op jit(solution)/shard_map/all_to_all | solution.py:882
  368.8 5.7 all-to-all-start.14
  374.5 4.5 add_convert_fusion
  379.0 17.9 %all-to-all-done.14 = bf16[64,48,256]{2,1,0:T(8,128)(2,1)} async-done(((bf16[64,48,256]{2,1,0:T(8,128)(2,1)}), bf16[64,48,256]{2,1,0:T(8,128)(2,1)}, u32[]{:S(2)}, u32[]{:S(2)}) %all-to-all-start.14) | async-done | bytes 1572896 | tf_op jit(solution)/shard_map/all_to_all | solution.py:889
  396.9 6.2 all-to-all-start.12
  408.0 11.5 %conv_back.3 = (f32[256,1792]{1,0:T(8,128)}, f32[8,1792]{1,0:T(8,128)S(1)}, f32[8,1792]{1,0:T(8,128)S(1)}, bf16[256,128]{1,0:T(8,128)(2,1)S(1)}, f32[8,128]{1,0:T(8,128)S(1)}) custom-call(bf16[1536,128]{1,0:T(8,128)(2,1)} %bitcast.16.later_ref, bf16[1536,128]{1,0:T(8,128)(2,1)} %bitcast.6.state_ref, f32[256,1536]{1,0:T(8,128)S(1)} %get-tuple-element.123.dv_ref, ...), custom_call_target="tpu_custom_call" | custom-call | flops 301989888 | bytes 12000000 | tf_op jit(solution)/shard_map/conv_back/pallas_call | solution.py:638
  423.6 9.9 %collective-permute-done.3.next_ref = f32[8,1792]{1,0:T(8,128)S(1)} collective-permute-done((f32[8,1792]{1,0:T(8,128)S(1)}, f32[8,1792]{1,0:T(8,128)S(1)}, u32[]{:S(2)}, u32[]{:S(2)}) %collective-permute-start.3) | collective-permute-done | bytes 57376 | tf_op jit(solution)/shard_map/ppermute | solution.py:878
  435.0 5.3 norm_back.3
  451.8 6.8 %all-to-all-start.15 = ((bf16[32,48,256]{2,1,0:T(8,128)(2,1)}), bf16[32,48,256]{2,1,0:T(8,128)(2,1)S(1)}, u32[]{:S(2)}, u32[]{:S(2)}) async-start(bf16[32,48,256]{2,1,0:T(8,128)(2,1)} %broadcast_in_dim.48), calls=%async_computation.15 | async-start | bytes 1572864 | tf_op jit(solution)/shard_map/all_to_all | solution.py:882
  462.1 10.7 %all-to-all-done.15 = bf16[32,48,256]{2,1,0:T(8,128)(2,1)S(1)} async-done(((bf16[32,48,256]{2,1,0:T(8,128)(2,1)}), bf16[32,48,256]{2,1,0:T(8,128)(2,1)S(1)}, u32[]{:S(2)}, u32[]{:S(2)}) %all-to-all-start.15) | async-done | bytes 786464 | tf_op jit(solution)/shard_map/all_to_all | solution.py:882
  472.8 5.8 all-to-all-start.10
  478.6 4.5 add_convert_fusion.1
  483.1 18.8 %all-to-all-done.10 = bf16[64,48,256]{2,1,0:T(8,128)(2,1)} async-done(((bf16[64,48,256]{2,1,0:T(8,128)(2,1)}), bf16[64,48,256]{2,1,0:T(8,128)(2,1)}, u32[]{:S(2)}, u32[]{:S(2)}) %all-to-all-start.10) | async-done | bytes 1572896 | tf_op jit(solution)/shard_map/all_to_all | solution.py:889
  501.9 5.6 all-to-all-start.8
  509.1 27.7 %all-to-all-done.8 = bf16[64,48,384]{2,1,0:T(8,128)(2,1)} async-done(((bf16[64,48,384]{2,1,0:T(8,128)(2,1)}), bf16[64,48,384]{2,1,0:T(8,128)(2,1)}, u32[]{:S(2)}, u32[]{:S(2)}) %all-to-all-start.8) | async-done | bytes 2359328 | tf_op jit(solution)/shard_map/all_to_all | solution.py:889
  537.8 8.1 %all-to-all-start.11 = ((bf16[32,48,256]{2,1,0:T(8,128)(2,1)}), bf16[32,48,256]{2,1,0:T(8,128)(2,1)S(1)}, u32[]{:S(2)}, u32[]{:S(2)}) async-start(bf16[32,48,256]{2,1,0:T(8,128)(2,1)} %broadcast_in_dim.46), calls=%async_computation.11 | async-start | bytes 1572864 | tf_op jit(solution)/shard_map/all_to_all | solution.py:882
  547.9 12.2 %all-to-all-done.11 = bf16[32,48,256]{2,1,0:T(8,128)(2,1)S(1)} async-done(((bf16[32,48,256]{2,1,0:T(8,128)(2,1)}), bf16[32,48,256]{2,1,0:T(8,128)(2,1)S(1)}, u32[]{:S(2)}, u32[]{:S(2)}) %all-to-all-start.11) | async-done | bytes 786464 | tf_op jit(solution)/shard_map/all_to_all | solution.py:882
  567.9 15.7 %all-to-all-done.13 = bf16[32,48,384]{2,1,0:T(8,128)(2,1)S(1)} async-done(((bf16[32,48,384]{2,1,0:T(8,128)(2,1)}), bf16[32,48,384]{2,1,0:T(8,128)(2,1)S(1)}, u32[]{:S(2)}, u32[]{:S(2)}) %all-to-all-start.13) | async-done | bytes 1179680 | tf_op jit(solution)/shard_map/all_to_all | solution.py:882
  585.5 4.5 all-to-all-start.9
  594.2 7.4 %adam_in.2 = (f32[2,192,3352]{2,1,0:T(8,128)}, f32[2,192,3352]{2,1,0:T(8,128)}, f32[2,192,3352]{2,1,0:T(8,128)}) custom-call(bf16[4,8,48,384]{3,2,1,0:T(8,128)(2,1)S(1)} %bitcast.46, bf16[4,8,48,256]{3,2,1,0:T(8,128)(2,1)S(1)} %bitcast.54, f32[2,192,3352]{2,1,0:T(8,128)} %w_ref.3, f32[2,192,3352]{2,1,0:T(8,128)} %m_ref.3, f32[2,192,3352]{2,1,0:T(8,128)} %v_ref.3), custom_call_target="tpu_custom_call" | custom-call | bytes 17000000 | tf_op jit(solution)/shard_map/adam_in/pallas_call | solution.py:820
  601.7 4.4 adam_out.2
  609.6 7.7 %adam_in.3 = (f32[2,192,3352]{2,1,0:T(8,128)}, f32[2,192,3352]{2,1,0:T(8,128)}, f32[2,192,3352]{2,1,0:T(8,128)}) custom-call(bf16[4,8,48,384]{3,2,1,0:T(8,128)(2,1)} %bitcast.20.zo_ref, bf16[4,8,48,256]{3,2,1,0:T(8,128)(2,1)S(1)} %bitcast.56, f32[2,192,3352]{2,1,0:T(8,128)} %w_ref.3, ...), custom_call_target="tpu_custom_call", output_to_operand_aliasing={{0}: (5, {}), {1}: (6, {}), {2}: (7, {})} | custom-call | bytes 17000000 | tf_op jit(solution)/shard_map/adam_in/pallas_call | solution.py:820
  617.3 4.6 adam_out.3
  (321 shorter events, 149.7 us)
Async XLA Ops:
  7.2 65.5 %all-gather.10.cloned.1.call-start = ((), (), s32[]{:S(2)}) async-start(), calls=%async_computation.16 | async-start | bytes 6635520 | tf_op jit(solution)/shard_map/all_gather | solution.py:903
  11.7 111.7 %all-gather.12.cloned.1.call-start = ((), (), s32[]{:S(2)}) async-start(), calls=%async_computation.17 | async-start | bytes 2949120 | tf_op jit(solution)/shard_map/all_gather | solution.py:904
  13.9 154.5 %all-gather.14.cloned.1.call-start = ((), (), s32[]{:S(2)}) async-start(), calls=%async_computation.18 | async-start | bytes 6635520 | tf_op jit(solution)/shard_map/all_gather | solution.py:903
  14.6 206.6 %all-gather.16.cloned.1.call-start = ((), (), s32[]{:S(2)}) async-start(), calls=%async_computation.19 | async-start | bytes 2949120 | tf_op jit(solution)/shard_map/all_gather | solution.py:904
  14.7 67.0 %collective-permute-start = (bf16[8,768]{1,0:T(8,128)(2,1)S(1)}, bf16[8,768]{1,0:T(8,128)(2,1)S(1)}, u32[]{:S(2)}, u32[]{:S(2)}) collective-permute-start(bf16[8,768]{1,0:T(8,128)(2,1)S(1)} %slice_bitcast_fusion), channel_id=1, source_target_pairs={{0,4},{4,8},{8,12},{12,16},{16,20},{20,24},{24,28},{28,32},{32,36}... | collective-permute-start | bytes 36872 | tf_op jit(solution)/shard_map/ppermute | solution.py:878
  29.4 43.3 %copy-start.119 = (f32[11336,2]{0,1:T(2,128)}, f32[11336,2]{0,1:T(2,128)S(1)}, u32[]{:S(2)}) copy-start(f32[11336,2]{0,1:T(2,128)S(1)} %reshape.132) | copy-start | bytes 272068
  29.6 52.1 %copy-start.61 = (f32[4,1792]{1,0:T(4,128)}, f32[4,1792]{1,0:T(4,128)S(1)}, u32[]{:S(2)}) copy-start(f32[4,1792]{1,0:T(4,128)S(1)} %squeeze.9.taps_ref) | copy-start | bytes 86020
  30.3 51.4 %copy-start.89 = (f32[1,128]{1,0:T(1,128)}, f32[1,128]{1,0:T(1,128)S(1)}, u32[]{:S(2)}) copy-start(f32[1,128]{1,0:T(1,128)S(1)} %get-tuple-element.191.dtb_ref) | copy-start | bytes 1540
  30.3 51.4 %copy-start.91 = (f32[1,128]{1,0:T(1,128)}, f32[1,128]{1,0:T(1,128)S(1)}, u32[]{:S(2)}) copy-start(f32[1,128]{1,0:T(1,128)S(1)} %get-tuple-element.194.decay_ref) | copy-start | bytes 1540
  30.3 148.8 %copy-start.93 = (f32[1,128]{1,0:T(1,128)}, f32[1,128]{1,0:T(1,128)S(1)}, u32[]{:S(2)}) copy-start(f32[1,128]{1,0:T(1,128)S(1)} %get-tuple-element.190.dtb_ref) | copy-start | bytes 1540
  30.3 51.4 %copy-start.82 = (f32[1,768]{1,0:T(1,128)}, f32[1,768]{1,0:T(1,128)S(1)}, u32[]{:S(2)}) copy-start(f32[1,768]{1,0:T(1,128)S(1)} %get-tuple-element.187.gain_ref) | copy-start | bytes 9220
  30.3 148.8 %copy-start.84 = (f32[1,768]{1,0:T(1,128)}, f32[1,768]{1,0:T(1,128)S(1)}, u32[]{:S(2)}) copy-start(f32[1,768]{1,0:T(1,128)S(1)} %get-tuple-element.186.gain_ref) | copy-start | bytes 9220
  93.5 19.4 %all-to-all-start = ((bf16[32,64,128]{2,1,0:T(8,128)(2,1)}), bf16[32,64,128]{2,1,0:T(8,128)(2,1)}, u32[]{:S(2)}, u32[]{:S(2)}) async-start(bf16[32,64,128]{2,1,0:T(8,128)(2,1)} %copy-done.54), calls=%async_computation | async-start | bytes 1048576 | tf_op jit(solution)/shard_map/all_to_all | solution.py:882
  115.2 14.5 %all-to-all-start.1 = ((bf16[32,48,128]{2,1,0:T(8,128)(2,1)}), bf16[32,48,128]{2,1,0:T(8,128)(2,1)}, u32[]{:S(2)}, u32[]{:S(2)}) async-start(bf16[32,48,128]{2,1,0:T(8,128)(2,1)} %copy-done.56), calls=%async_computation.1 | async-start | bytes 786432 | tf_op jit(solution)/shard_map/all_to_all | solution.py:882
  139.4 39.1 %collective-permute-start.1 = (f32[8,768]{1,0:T(8,128)S(1)}, f32[8,768]{1,0:T(8,128)S(1)}, u32[]{:S(2)}, u32[]{:S(2)}) collective-permute-start(f32[8,768]{1,0:T(8,128)S(1)} %slice.140), channel_id=1, source_target_pairs={{0,4},{4,8},{8,12},{12,16},{16,20},{20,24},{24,28},{28,32},{32,36}... | collective-permute-start | bytes 73736 | tf_op jit(solution)/shard_map/ppermute | solution.py:878
  169.5 9.7 %copy-start.59 = (f32[4,1792]{1,0:T(4,128)S(1)}, f32[4,1792]{1,0:T(4,128)}, u32[]{:S(2)}) copy-start(f32[4,1792]{1,0:T(4,128)} %squeeze.20.taps_ref) | copy-start | bytes 86020
  169.5 9.7 %copy-start.86 = (f32[1,1792]{1,0:T(1,128)S(1)}, f32[1,1792]{1,0:T(1,128)}, u32[]{:S(2)}) copy-start(f32[1,1792]{1,0:T(1,128)} %get-tuple-element.184.bias_ref) | copy-start | bytes 21508
  169.5 9.7 %copy-start.95 = (f32[1,128]{1,0:T(1,128)S(1)}, f32[1,128]{1,0:T(1,128)}, u32[]{:S(2)}) copy-start(f32[1,128]{1,0:T(1,128)} %get-tuple-element.195.decay_ref) | copy-start | bytes 1540
  190.5 19.6 %copy-start.65 = (f32[256,128]{1,0:T(8,128)}, f32[256,128]{1,0:T(8,128)S(1)}, u32[]{:S(2)}) copy-start(f32[256,128]{1,0:T(8,128)S(1)} %get-tuple-element.111.step_ref) | copy-start | bytes 393220
  190.5 19.7 %copy-start.77 = (f32[8,1792]{1,0:T(8,128)}, f32[8,1792]{1,0:T(8,128)S(1)}, u32[]{:S(2)}) copy-start(f32[8,1792]{1,0:T(8,128)S(1)} %get-tuple-element.110.edge_ref) | copy-start | bytes 172036
  190.5 25.7 %copy-start.121 = (f32[24]{0:T(128)S(1)}, f32[24]{0:T(128)}, u32[]{:S(2)}) copy-start(f32[24]{0:T(128)} %get-tuple-element.180) | copy-start | bytes 292
  211.5 14.7 %all-to-all-start.3 = ((bf16[32,48,128]{2,1,0:T(8,128)(2,1)}), bf16[32,48,128]{2,1,0:T(8,128)(2,1)}, u32[]{:S(2)}, u32[]{:S(2)}) async-start(bf16[32,48,128]{2,1,0:T(8,128)(2,1)} %copy-done.55), calls=%async_computation.3 | async-start | bytes 786432 | tf_op jit(solution)/shard_map/all_to_all | solution.py:882
  238.0 24.6 %copy-start.74 = (f32[128,128]{1,0:T(8,128)S(1)}, f32[128,128]{1,0:T(8,128)}, u32[]{:S(2)}) copy-start(f32[128,128]{1,0:T(8,128)} %copy-done.73) | copy-start | bytes 196612
  249.0 13.6 %copy-start.46 = (bf16[256,1536]{1,0:T(8,128)(2,1)}, bf16[256,1536]{1,0:T(8,128)(2,1)S(1)}, u32[]{:S(2)}) copy-start(bf16[256,1536]{1,0:T(8,128)(2,1)S(1)} %get-tuple-element.108.dy_ref) | copy-start | bytes 2359300
  263.7 14.9 %all-to-all-start.5 = ((bf16[32,48,128]{2,1,0:T(8,128)(2,1)}), bf16[32,48,128]{2,1,0:T(8,128)(2,1)}, u32[]{:S(2)}, u32[]{:S(2)}) async-start(bf16[32,48,128]{2,1,0:T(8,128)(2,1)} %copy-done.35), calls=%async_computation.5 | async-start | bytes 786432 | tf_op jit(solution)/shard_map/all_to_all | solution.py:882
  301.2 5.7 collective-permute-start.2
  317.6 9.2 %copy-start.24 = (f32[256,768]{1,0:T(8,128)}, f32[256,768]{1,0:T(8,128)S(1)}, u32[]{:S(2)}) copy-start(f32[256,768]{1,0:T(8,128)S(1)} %get-tuple-element.118.grad_ref) | copy-start | bytes 2359300
  321.4 37.2 %collective-permute-start.7 = (bf16[16,4,48,256]{3,2,1,0:T(8,128)(2,1)}, bf16[16,4,48,256]{3,2,1,0:T(8,128)(2,1)}, u32[]{:S(2)}, u32[]{:S(2)}) collective-permute-start(bf16[16,4,48,256]{3,2,1,0:T(8,128)(2,1)} %get-tuple-element.158), channel_id=1, source_target_pairs={{0,4},{4,0},{1,5},{5,1},{2,6},{6,2},{3,7},{7,3},{8,12},{12,8},{9,1... | collective-permute-start | bytes 4718600 | tf_op jit(solution)/shard_map/ppermute | solution.py:886
  326.1 48.4 %collective-permute-start.6 = (bf16[16,4,48,384]{3,2,1,0:T(8,128)(2,1)}, bf16[16,4,48,384]{3,2,1,0:T(8,128)(2,1)}, u32[]{:S(2)}, u32[]{:S(2)}) collective-permute-start(bf16[16,4,48,384]{3,2,1,0:T(8,128)(2,1)} %get-tuple-element.150), channel_id=1, source_target_pairs={{0,4},{4,0},{1,5},{5,1},{2,6},{6,2},{3,7},{7,3},{8,12},{12,8},{9,1... | collective-permute-start | bytes 7077896 | tf_op jit(solution)/shard_map/ppermute | solution.py:886
  326.8 26.4 %copy-start.72 = (f32[128,128]{1,0:T(8,128)S(1)}, f32[128,128]{1,0:T(8,128)}, u32[]{:S(2)}) copy-start(f32[128,128]{1,0:T(8,128)} %copy-done.71) | copy-start | bytes 196612
  336.5 16.6 %copy-start.43 = (bf16[256,1536]{1,0:T(8,128)(2,1)}, bf16[256,1536]{1,0:T(8,128)(2,1)S(1)}, u32[]{:S(2)}) copy-start(bf16[256,1536]{1,0:T(8,128)(2,1)S(1)} %get-tuple-element.122.dy_ref) | copy-start | bytes 2359300
  354.2 14.5 %all-to-all-start.7 = ((bf16[32,48,128]{2,1,0:T(8,128)(2,1)}), bf16[32,48,128]{2,1,0:T(8,128)(2,1)}, u32[]{:S(2)}, u32[]{:S(2)}) async-start(bf16[32,48,128]{2,1,0:T(8,128)(2,1)} %copy-done.34), calls=%async_computation.7 | async-start | bytes 786432 | tf_op jit(solution)/shard_map/all_to_all | solution.py:882
  368.8 28.2 %all-to-all-start.14 = ((bf16[64,48,256]{2,1,0:T(8,128)(2,1)}), bf16[64,48,256]{2,1,0:T(8,128)(2,1)}, u32[]{:S(2)}, u32[]{:S(2)}) async-start(bf16[64,48,256]{2,1,0:T(8,128)(2,1)} %bitcast.73), calls=%async_computation.14 | async-start | bytes 3145728 | tf_op jit(solution)/shard_map/all_to_all | solution.py:889
  396.9 54.0 %all-to-all-start.12 = ((bf16[64,48,384]{2,1,0:T(8,128)(2,1)}), bf16[64,48,384]{2,1,0:T(8,128)(2,1)}, u32[]{:S(2)}, u32[]{:S(2)}) async-start(bf16[64,48,384]{2,1,0:T(8,128)(2,1)} %bitcast.65), calls=%async_computation.12 | async-start | bytes 4718592 | tf_op jit(solution)/shard_map/all_to_all | solution.py:889
  408.0 25.5 %copy-start.19 = (bf16[1,256,768]{2,1,0:T(8,128)(2,1)S(1)}, bf16[1,256,768]{2,1,0:T(8,128)(2,1)}, u32[]{:S(2)}) copy-start(bf16[1,256,768]{2,1,0:T(8,128)(2,1)} %param.11) | copy-start | bytes 1179652
  408.0 25.5 %copy-start.25 = (f32[256,768]{1,0:T(8,128)S(1)}, f32[256,768]{1,0:T(8,128)}, u32[]{:S(2)}) copy-start(f32[256,768]{1,0:T(8,128)} %copy-done.24) | copy-start | bytes 2359300
  408.0 25.5 %copy-start.50 = (bf16[256,1536]{1,0:T(8,128)(2,1)S(1)}, bf16[256,1536]{1,0:T(8,128)(2,1)}, u32[]{:S(2)}) copy-start(bf16[256,1536]{1,0:T(8,128)(2,1)} %copy-done.49) | copy-start | bytes 2359300
  408.0 25.4 %copy-start.83 = (f32[1,768]{1,0:T(1,128)S(1)}, f32[1,768]{1,0:T(1,128)}, u32[]{:S(2)}) copy-start(f32[1,768]{1,0:T(1,128)} %copy-done.82) | copy-start | bytes 9220
  419.5 13.9 %collective-permute-start.3 = (f32[8,1792]{1,0:T(8,128)S(1)}, f32[8,1792]{1,0:T(8,128)S(1)}, u32[]{:S(2)}, u32[]{:S(2)}) collective-permute-start(f32[8,1792]{1,0:T(8,128)S(1)} %get-tuple-element.129), channel_id=1, source_target_pairs={{4,0},{8,4},{12,8},{16,12},{20,16},{24,20},{28,24},{32,28},{36,32}... | collective-permute-start | bytes 172040 | tf_op jit(solution)/shard_map/ppermute | solution.py:878
  444.1 14.5 %collective-permute-start.5 = (bf16[16,4,48,256]{3,2,1,0:T(8,128)(2,1)}, bf16[16,4,48,256]{3,2,1,0:T(8,128)(2,1)}, u32[]{:S(2)}, u32[]{:S(2)}) collective-permute-start(bf16[16,4,48,256]{3,2,1,0:T(8,128)(2,1)} %get-tuple-element.145), channel_id=1, source_target_pairs={{0,4},{4,0},{1,5},{5,1},{2,6},{6,2},{3,7},{7,3},{8,12},{12,8},{9,1... | collective-permute-start | bytes 4718600 | tf_op jit(solution)/shard_map/ppermute | solution.py:886
  448.7 29.9 %collective-permute-start.4 = (bf16[16,4,48,384]{3,2,1,0:T(8,128)(2,1)}, bf16[16,4,48,384]{3,2,1,0:T(8,128)(2,1)}, u32[]{:S(2)}, u32[]{:S(2)}) collective-permute-start(bf16[16,4,48,384]{3,2,1,0:T(8,128)(2,1)} %get-tuple-element.137), channel_id=1, source_target_pairs={{0,4},{4,0},{1,5},{5,1},{2,6},{6,2},{3,7},{7,3},{8,12},{12,8},{9,1... | collective-permute-start | bytes 7077896 | tf_op jit(solution)/shard_map/ppermute | solution.py:886
  451.8 21.0 %all-to-all-start.15 = ((bf16[32,48,256]{2,1,0:T(8,128)(2,1)}), bf16[32,48,256]{2,1,0:T(8,128)(2,1)S(1)}, u32[]{:S(2)}, u32[]{:S(2)}) async-start(bf16[32,48,256]{2,1,0:T(8,128)(2,1)} %broadcast_in_dim.48), calls=%async_computation.15 | async-start | bytes 1572864 | tf_op jit(solution)/shard_map/all_to_all | solution.py:882
  472.8 10.3 %copy-start.20 = (bf16[32,48,256]{2,1,0:T(8,128)(2,1)}, bf16[32,48,256]{2,1,0:T(8,128)(2,1)S(1)}, u32[]{:S(2)}) copy-start(bf16[32,48,256]{2,1,0:T(8,128)(2,1)S(1)} %all-to-all-done.15) | copy-start | bytes 2359300
  472.8 29.1 %all-to-all-start.10 = ((bf16[64,48,256]{2,1,0:T(8,128)(2,1)}), bf16[64,48,256]{2,1,0:T(8,128)(2,1)}, u32[]{:S(2)}, u32[]{:S(2)}) async-start(bf16[64,48,256]{2,1,0:T(8,128)(2,1)} %bitcast.74), calls=%async_computation.10 | async-start | bytes 3145728 | tf_op jit(solution)/shard_map/all_to_all | solution.py:889
  501.9 34.9 %all-to-all-start.8 = ((bf16[64,48,384]{2,1,0:T(8,128)(2,1)}), bf16[64,48,384]{2,1,0:T(8,128)(2,1)}, u32[]{:S(2)}, u32[]{:S(2)}) async-start(bf16[64,48,384]{2,1,0:T(8,128)(2,1)} %bitcast.66), calls=%async_computation.8 | async-start | bytes 4718592 | tf_op jit(solution)/shard_map/all_to_all | solution.py:889
  537.8 22.3 %all-to-all-start.11 = ((bf16[32,48,256]{2,1,0:T(8,128)(2,1)}), bf16[32,48,256]{2,1,0:T(8,128)(2,1)S(1)}, u32[]{:S(2)}, u32[]{:S(2)}) async-start(bf16[32,48,256]{2,1,0:T(8,128)(2,1)} %broadcast_in_dim.46), calls=%async_computation.11 | async-start | bytes 1572864 | tf_op jit(solution)/shard_map/all_to_all | solution.py:882
  561.4 22.2 %all-to-all-start.13 = ((bf16[32,48,384]{2,1,0:T(8,128)(2,1)}), bf16[32,48,384]{2,1,0:T(8,128)(2,1)S(1)}, u32[]{:S(2)}, u32[]{:S(2)}) async-start(bf16[32,48,384]{2,1,0:T(8,128)(2,1)} %broadcast_in_dim.47), calls=%async_computation.13 | async-start | bytes 2359296 | tf_op jit(solution)/shard_map/all_to_all | solution.py:882
  585.5 23.0 %all-to-all-start.9 = ((bf16[32,48,384]{2,1,0:T(8,128)(2,1)}), bf16[32,48,384]{2,1,0:T(8,128)(2,1)}, u32[]{:S(2)}, u32[]{:S(2)}) async-start(bf16[32,48,384]{2,1,0:T(8,128)(2,1)} %broadcast_in_dim.45), calls=%async_computation.9 | async-start | bytes 2359296 | tf_op jit(solution)/shard_map/all_to_all | solution.py:882
  (99 other events, 210.2 us)
Sparse Core Ops, SparseCore 0:
  11.8 60.8 all-gather.9
  75.0 33.4 all-gather.11
  110.7 57.5 all-gather.13
  170.4 33.5 all-gather.15
